TPU v7x, 32 devices: a whole 2x2x4 slice. The times are simulated.
32 devices in a mesh: sp: 8 (over z, y), dp: 4 (over x, core).
Axes of the slice: x: 2, y: 2, z: 4, core: 2. Of those that a mesh axis runs over, the one named last changes fastest.
Arguments:
- queries: bfloat16 [4096, 8192], P(('dp', 'sp')), parts along dimension 0, may hold values from -60 to 60
- key_heads: bfloat16 [4096, 1024], P(('dp', 'sp')), parts along dimension 0, may hold values from -6 to 6
- value_heads: bfloat16 [4096, 1024], P(('dp', 'sp')), parts along dimension 0, may hold values from -6 to 6
- out_grad: bfloat16 [4096, 8192], P(('dp', 'sp')), parts along dimension 0, may hold values from -6 to 6
- segment_ids: int32 [4096], P(('dp', 'sp')), parts along dimension 0, may hold values from 0 to 3, never falling along the last dimension, each value on 1 to 512 neighbouring positions
Outputs:
- d_query: bfloat16 [4096, 8192], P(('dp', 'sp')), parts along dimension 0
- d_key: bfloat16 [4096, 1024], P(('dp', 'sp')), parts along dimension 0
- d_value: bfloat16 [4096, 1024], P(('dp', 'sp')), parts along dimension 0
There are 4 independent parts, one for each index of `dp`. A program takes and returns all parts, laid end to end along the dimension named above; each array names one. Nothing has to cross between parts.
Inputs may be any that keep to these rules, and one draw needn't show every extreme that they name: `segment_ids`: documents are runs of consecutive tokens with rising ids, each of at most 512 tokens; one has exactly 512.
All inputs are finite; a program needn't handle non-finite values.
Results may differ from a plain program's by a relative error of at most 0.0065.
Values may be sent and summed in bfloat16 or wider, within the bound.
A program may use at most 192 MiB of HBM per device.

v0:
```python
import jax
import jax.numpy as jnp
from jax import lax
from jax.sharding import PartitionSpec as P

HEAD_DIM = 128
MOST = 512


def grad_core(query_part, grad_part, key_part, value_part, allowed, scale):
    scores = (
        jnp.einsum("kgqd,kjd->kgqj", query_part, key_part, preferred_element_type=jnp.float32)
        * scale
    )
    scores = jnp.where(allowed, scores, -1e30)
    row_max = jnp.max(scores, axis=-1, keepdims=True)
    probs = jnp.exp(scores - row_max)
    probs = probs / jnp.sum(probs, axis=-1, keepdims=True)
    probs_low = probs.astype(jnp.bfloat16)
    prob_grads = jnp.einsum(
        "kgqd,kjd->kgqj", grad_part, value_part, preferred_element_type=jnp.float32
    )
    delta = jnp.sum(probs * prob_grads, axis=-1, keepdims=True)
    score_grads = (probs * (prob_grads - delta)).astype(jnp.bfloat16)
    query_grad = (
        jnp.einsum("kgqj,kjd->kgqd", score_grads, key_part, preferred_element_type=jnp.float32)
        * scale
    )
    key_grad = (
        jnp.einsum("kgqj,kgqd->kjd", score_grads, query_part, preferred_element_type=jnp.float32)
        * scale
    )
    value_grad = jnp.einsum(
        "kgqj,kgqd->kjd", probs_low, grad_part, preferred_element_type=jnp.float32
    )
    return (query_grad, key_grad, value_grad)


def body(queries, key_heads, value_heads, out_grad, segment_ids):
    scale = HEAD_DIM ** (-0.5)
    tokens, width = queries.shape
    kv_width = key_heads.shape[1]
    kv_count = kv_width // HEAD_DIM
    group = width // kv_width
    devices = lax.axis_size("sp")
    all_ids = lax.all_gather(segment_ids, "sp", axis=0, tiled=True)
    seq_len = tokens * devices
    local = width // HEAD_DIM // devices
    block = min(512, seq_len)
    span = MOST + block
    keys_wide = jnp.broadcast_to(
        key_heads.reshape(tokens, kv_count, 1, HEAD_DIM), (tokens, kv_count, group, HEAD_DIM)
    ).reshape(tokens, width)
    values_wide = jnp.broadcast_to(
        value_heads.reshape(tokens, kv_count, 1, HEAD_DIM), (tokens, kv_count, group, HEAD_DIM)
    ).reshape(tokens, width)
    moved = (
        lax.all_to_all(queries, "sp", split_axis=1, concat_axis=0, tiled=True),
        lax.all_to_all(out_grad, "sp", split_axis=1, concat_axis=0, tiled=True),
        lax.all_to_all(keys_wide, "sp", split_axis=1, concat_axis=0, tiled=True),
        lax.all_to_all(values_wide, "sp", split_axis=1, concat_axis=0, tiled=True),
    )
    local_q = moved[0].reshape(seq_len, local, HEAD_DIM)
    local_g = moved[1].reshape(seq_len, local, HEAD_DIM)
    filler = jnp.zeros((MOST, local, HEAD_DIM), jnp.bfloat16)
    keys_pad = jnp.concatenate([filler, moved[2].reshape(seq_len, local, HEAD_DIM)], axis=0)
    values_pad = jnp.concatenate([filler, moved[3].reshape(seq_len, local, HEAD_DIM)], axis=0)
    ids_pad = jnp.concatenate([jnp.full((MOST,), -1, jnp.int32), all_ids], axis=0)

    def one_block(carry, number):
        key_acc, value_acc = carry
        start = number * block
        q_blk = lax.dynamic_slice_in_dim(local_q, start, block, 0).transpose(1, 0, 2)[:, None]
        g_blk = lax.dynamic_slice_in_dim(local_g, start, block, 0).transpose(1, 0, 2)[:, None]
        k_win = lax.dynamic_slice_in_dim(keys_pad, start, span, 0).transpose(1, 0, 2)
        v_win = lax.dynamic_slice_in_dim(values_pad, start, span, 0).transpose(1, 0, 2)
        ids_q = lax.dynamic_slice_in_dim(all_ids, start, block, 0)
        ids_k = lax.dynamic_slice_in_dim(ids_pad, start, span, 0)
        q_pos = start + jnp.arange(block, dtype=jnp.int32)
        k_pos = start - MOST + jnp.arange(span, dtype=jnp.int32)
        allowed = (ids_q[:, None] == ids_k[None, :]) & (k_pos[None, :] <= q_pos[:, None])
        query_grad, key_grad, value_grad = grad_core(q_blk, g_blk, k_win, v_win, allowed, scale)
        old_key = lax.dynamic_slice_in_dim(key_acc, start, span, 0)
        old_value = lax.dynamic_slice_in_dim(value_acc, start, span, 0)
        key_acc = lax.dynamic_update_slice_in_dim(
            key_acc, old_key + key_grad.transpose(1, 0, 2), start, 0
        )
        value_acc = lax.dynamic_update_slice_in_dim(
            value_acc, old_value + value_grad.transpose(1, 0, 2), start, 0
        )
        return ((key_acc, value_acc), query_grad[:, 0].transpose(1, 0, 2).astype(jnp.bfloat16))

    zeros_acc = jnp.zeros((seq_len + MOST, local, HEAD_DIM), jnp.float32)
    (key_acc, value_acc), query_blocks = lax.scan(
        one_block, (zeros_acc, zeros_acc), jnp.arange(seq_len // block, dtype=jnp.int32)
    )
    query_seq = query_blocks.reshape(seq_len, local * HEAD_DIM)
    key_seq = key_acc[MOST:].reshape(seq_len, local * HEAD_DIM)
    value_seq = value_acc[MOST:].reshape(seq_len, local * HEAD_DIM)
    d_query = lax.all_to_all(query_seq, "sp", split_axis=0, concat_axis=1, tiled=True)
    key_back, value_back = (
        lax.all_to_all(key_seq, "sp", split_axis=0, concat_axis=1, tiled=True),
        lax.all_to_all(value_seq, "sp", split_axis=0, concat_axis=1, tiled=True),
    )
    d_key = (
        key_back.reshape(tokens, kv_count, group, HEAD_DIM)
        .sum(axis=2)
        .reshape(tokens, kv_width)
        .astype(jnp.bfloat16)
    )
    d_value = (
        value_back.reshape(tokens, kv_count, group, HEAD_DIM)
        .sum(axis=2)
        .reshape(tokens, kv_width)
        .astype(jnp.bfloat16)
    )
    return (d_query, d_key, d_value)


def solution(mesh):
    placed = (
        P(("dp", "sp"), None),
        P(("dp", "sp"), None),
        P(("dp", "sp"), None),
        P(("dp", "sp"), None),
        P(("dp", "sp")),
    )
    return jax.shard_map(
        body,
        mesh=mesh,
        in_specs=placed,
        out_specs=(P(("dp", "sp"), None), P(("dp", "sp"), None), P(("dp", "sp"), None)),
        check_vma=False,
    )
```

profile of v0, /device:TPU:0, one launch (start us, length us, event | category | flops | bytes accessed | tf_op | source)
XLA Modules:
  0.0 689.9 jit_solution(8003659729316231698)
XLA Ops:
  0.6 0.9 copy-done
  1.9 2.3 all_to_all.89
  4.2 7.3 %all-to-all-start.1 = ((bf16[128,8,1024]{2,0,1:T(8,128)(2,1)}), bf16[128,8,1024]{2,0,1:T(8,128)(2,1)S(1)}, u32[]{:S(2)}, u32[]{:S(2)}) async-start(bf16[128,8,1024]{2,0,1:T(8,128)(2,1)} %all_to_all.89), calls=%async_computation.1 | async-start | bytes 4194304 | tf_op jit(solution)/shard_map/all_to_all | solution.py:60
  11.6 1.7 broadcast_in_dim.51
  13.2 4.2 all_to_all.95
  17.4 42.4 %all-to-all-done.1 = bf16[128,8,1024]{2,0,1:T(8,128)(2,1)S(1)} async-done(((bf16[128,8,1024]{2,0,1:T(8,128)(2,1)}), bf16[128,8,1024]{2,0,1:T(8,128)(2,1)S(1)}, u32[]{:S(2)}, u32[]{:S(2)}) %all-to-all-start.1) | async-done | bytes 2097184 | tf_op jit(solution)/shard_map/all_to_all | solution.py:60
  59.7 4.4 all-to-all-start.3
  64.1 3.2 copy.119
  67.3 44.7 %all-to-all-done.3 = bf16[128,8,1024]{2,0,1:T(8,128)(2,1)} async-done(((bf16[128,8,1024]{2,0,1:T(8,128)(2,1)}), bf16[128,8,1024]{2,0,1:T(8,128)(2,1)}, u32[]{:S(2)}, u32[]{:S(2)}) %all-to-all-start.3) | async-done | bytes 2097184 | tf_op jit(solution)/shard_map/all_to_all | solution.py:61
  111.9 4.3 all-to-all-start
  116.3 3.2 copy.118
  119.5 44.6 %all-to-all-done = bf16[128,8,1024]{2,0,1:T(8,128)(2,1)} async-done(((bf16[128,8,1024]{2,0,1:T(8,128)(2,1)}), bf16[128,8,1024]{2,0,1:T(8,128)(2,1)}, u32[]{:S(2)}, u32[]{:S(2)}) %all-to-all-start) | async-done | bytes 2097184 | tf_op jit(solution)/shard_map/all_to_all | solution.py:58
  164.1 4.4 all-to-all-start.2
  168.5 48.4 %all-gather = s32[8,1,128]{2,1,0:T(1,128)S(1)} all-gather(s32[1,1,128]{2,1,0:T(1,128)S(1)} %bitcast.145), channel_id=1, replica_groups=mesh['sp'=8,'dp'=4] {'sp'}, dimensions={0}, use_global_device_ids=true | all-gather | bytes 4608 | tf_op jit(solution)/shard_map/all_gather | solution.py:46
  217.5 2.2 copy.89
  219.7 5.0 concatenate.10
  224.7 5.0 concatenate.11
  229.7 3.6 copy.86
  233.3 3.5 copy.88
  236.8 3.1 broadcast_in_dim.46
  240.0 3.1 broadcast_in_dim.46.clone
  243.0 182.4 %while.16 = (s32[]{:T(128)}, f32[1536,8,128]{2,0,1:T(8,128)}, f32[1536,8,128]{2,0,1:T(8,128)}, bf16[2,512,8,128]{3,2,1,0:T(8,128)(2,1)}, s32[2]{0:T(128)S(1)}, /...) while((s32[]{:T(128)}, f32[1536,8,128]{2,0,1:T(8,128)}, ...), condition=%wide.region_4.5_spmd, body=%wide.region_0.4_spmd.sunk | while | flops 5437389312 | bytes 220330320 | solution.py:94
  244.5 3.8 constant_dynamic-slice_fusion.6
  248.3 2.7 constant_dynamic-slice_fusion.7
  251.0 8.1 %fusion.33 = f32[8,512,1024]{2,1,0:T(8,128)} fusion(bf16[1024,8,128]{2,1,0:T(8,128)(2,1)S(1)} %get-tuple-element.303, bf16[512,8,128]{2,1,0:T(8,128)(2,1)S(1)} %get-tuple-element.304), kind=kOutput, calls=%fused_computation.22.clone.1 | convolution fusion | flops 1073741824 | bytes 19922944 | tf_op jit(solution)/shard_map/while/body/eval_jaxpr/kgqd,kjd->kgqj/dot_general | solution.py:12
  259.2 1.3 compare_and_fusion.2
  260.6 21.7 %fusion.34 = (f32[8,512]{1,0:T(8,128)S(1)}, f32[8,512,1024]{2,1,0:T(8,128)}) fusion(f32[8,512,1024]{2,1,0:T(8,128)} %fusion.33, pred[512,1024]{1,0:T(8,128)(4,1)} %compare_and_fusion.2), kind=kOutput, calls=%fused_computation.39.clone.1 | output fusion | flops 25166848 | bytes 34095104 | tf_op jit(solution)/shard_map/while/body/eval_jaxpr/sub | solution.py:17
  282.3 12.9 %fusion.36 = f32[1536,8,128]{2,0,1:T(8,128)} fusion(f32[1536,8,128]{2,0,1:T(8,128)} %get-tuple-element.330, s32[]{:T(128)S(6)} %select_n.42, bf16[512,8,128]{2,1,0:T(8,128)(2,1)} %get-tuple-element.308, f32[8,512,1024]{2,1,0:T(8,128)} %get-tuple-element.305, f32[8,512]{1,0:T(8,128)S(1)} %get-tuple-element.306), kind=kOutput, calls=%fused_computation.13.clone.1 | convolution fusion | flops 1083179008 | bytes 26230788 | tf_op jit(solution)/shard_map/while/body/eval_jaxpr/kgqj,kgqd->kjd/dot_general | solution.py:33
  295.2 11.9 %multiply_reduce_fusion.2 = (f32[8,512]{1,0:T(8,128)S(1)}, f32[8,512,1024]{2,1,0:T(8,128)}) fusion(f32[8,512,1024]{2,1,0:T(8,128)} %get-tuple-element.305, f32[8,512]{1,0:T(8,128)S(1)} %get-tuple-element.306, bf16[1024,8,128]{2,1,0:T(8,128)(2,1)} %get-tuple-element.307, bf16[512,8,128]{2,1,0:T(8,128)(2,1)} %get-tuple-element.308), kind=kOutput, calls=%fused_computation.2.clone.1 | convolution fusion | flops 1086320640 | bytes 36732928 | tf_op jit(solution)/shard_map/while/body/eval_jaxpr/kgqd,kjd->kgqj/dot_general | solution.py:20
  307.1 11.5 %multiply_convert_fusion.3 = bf16[8,512,1024]{2,1,0:T(8,128)(2,1)S(1)} fusion(f32[8,512,1024]{2,1,0:T(8,128)} %get-tuple-element.309, f32[8,512]{1,0:T(8,128)S(1)} %get-tuple-element.310, f32[8,512,1024]{2,1,0:T(8,128)} %get-tuple-element.305, f32[8,512]{1,0:T(8,128)S(1)} %get-tuple-element.306), kind=kLoop, calls=%fused_computation.1.clone.1 | loop fusion | flops 16777216 | bytes 41975808 | tf_op jit(solution)/shard_map/while/body/eval_jaxpr/convert_element_type | solution.py:24
  318.7 2.3 fusion.37
  321.8 1.3 copy-done.3
  323.1 6.9 %fusion.35 = f32[1536,8,128]{2,0,1:T(8,128)} fusion(f32[1536,8,128]{2,0,1:T(8,128)} %get-tuple-element.329, s32[]{:T(128)S(6)} %select_n.42, bf16[8,512,1024]{2,1,0:T(8,128)(2,1)S(1)} %multiply_convert_fusion.3, bf16[512,8,128]{2,1,0:T(8,128)(2,1)S(1)} %get-tuple-element.304), kind=kOutput, calls=%fused_computation.15.clone.1 | convolution fusion | flops 1075838976 | bytes 17825796 | tf_op jit(solution)/shard_map/while/body/eval_jaxpr/kgqj,kgqd->kjd/dot_general | solution.py:30
  331.3 3.8 constant_dynamic-slice_fusion.6
  335.1 2.7 constant_dynamic-slice_fusion.7
  337.7 8.1 %fusion.33 = f32[8,512,1024]{2,1,0:T(8,128)} fusion(bf16[1024,8,128]{2,1,0:T(8,128)(2,1)S(1)} %get-tuple-element.303, bf16[512,8,128]{2,1,0:T(8,128)(2,1)S(1)} %get-tuple-element.304), kind=kOutput, calls=%fused_computation.22.clone.1 | convolution fusion | flops 1073741824 | bytes 19922944 | tf_op jit(solution)/shard_map/while/body/eval_jaxpr/kgqd,kjd->kgqj/dot_general | solution.py:12
  346.0 1.3 compare_and_fusion.2
  347.3 21.7 %fusion.34 = (f32[8,512]{1,0:T(8,128)S(1)}, f32[8,512,1024]{2,1,0:T(8,128)}) fusion(f32[8,512,1024]{2,1,0:T(8,128)} %fusion.33, pred[512,1024]{1,0:T(8,128)(4,1)} %compare_and_fusion.2), kind=kOutput, calls=%fused_computation.39.clone.1 | output fusion | flops 25166848 | bytes 34095104 | tf_op jit(solution)/shard_map/while/body/eval_jaxpr/sub | solution.py:17
  369.1 12.9 %fusion.36 = f32[1536,8,128]{2,0,1:T(8,128)} fusion(f32[1536,8,128]{2,0,1:T(8,128)} %get-tuple-element.330, s32[]{:T(128)S(6)} %select_n.42, bf16[512,8,128]{2,1,0:T(8,128)(2,1)} %get-tuple-element.308, f32[8,512,1024]{2,1,0:T(8,128)} %get-tuple-element.305, f32[8,512]{1,0:T(8,128)S(1)} %get-tuple-element.306), kind=kOutput, calls=%fused_computation.13.clone.1 | convolution fusion | flops 1083179008 | bytes 26230788 | tf_op jit(solution)/shard_map/while/body/eval_jaxpr/kgqj,kgqd->kjd/dot_general | solution.py:33
  382.0 11.9 %multiply_reduce_fusion.2 = (f32[8,512]{1,0:T(8,128)S(1)}, f32[8,512,1024]{2,1,0:T(8,128)}) fusion(f32[8,512,1024]{2,1,0:T(8,128)} %get-tuple-element.305, f32[8,512]{1,0:T(8,128)S(1)} %get-tuple-element.306, bf16[1024,8,128]{2,1,0:T(8,128)(2,1)} %get-tuple-element.307, bf16[512,8,128]{2,1,0:T(8,128)(2,1)} %get-tuple-element.308), kind=kOutput, calls=%fused_computation.2.clone.1 | convolution fusion | flops 1086320640 | bytes 36732928 | tf_op jit(solution)/shard_map/while/body/eval_jaxpr/kgqd,kjd->kgqj/dot_general | solution.py:20
  393.8 11.5 %multiply_convert_fusion.3 = bf16[8,512,1024]{2,1,0:T(8,128)(2,1)S(1)} fusion(f32[8,512,1024]{2,1,0:T(8,128)} %get-tuple-element.309, f32[8,512]{1,0:T(8,128)S(1)} %get-tuple-element.310, f32[8,512,1024]{2,1,0:T(8,128)} %get-tuple-element.305, f32[8,512]{1,0:T(8,128)S(1)} %get-tuple-element.306), kind=kLoop, calls=%fused_computation.1.clone.1 | loop fusion | flops 16777216 | bytes 41975808 | tf_op jit(solution)/shard_map/while/body/eval_jaxpr/convert_element_type | solution.py:24
  405.4 2.3 fusion.37
  408.5 1.3 copy-done.3
  409.8 6.9 fusion.35
  425.4 4.2 all_to_all.98
  429.6 11.0 %all-to-all-start.4 = ((bf16[8,128,1024]{2,1,0:T(8,128)(2,1)}), bf16[8,128,1024]{2,1,0:T(8,128)(2,1)S(1)}, u32[]{:S(2)}, u32[]{:S(2)}) async-start(bf16[8,128,1024]{2,1,0:T(8,128)(2,1)} %all_to_all.98), calls=%async_computation.4 | async-start | bytes 4194304 | tf_op jit(solution)/shard_map/all_to_all | solution.py:100
  440.6 2.5 slice.6
  443.0 4.4 copy.65
  447.4 4.9 all_to_all.102
  452.3 33.9 %all-to-all-done.4 = bf16[8,128,1024]{2,1,0:T(8,128)(2,1)S(1)} async-done(((bf16[8,128,1024]{2,1,0:T(8,128)(2,1)}), bf16[8,128,1024]{2,1,0:T(8,128)(2,1)S(1)}, u32[]{:S(2)}, u32[]{:S(2)}) %all-to-all-start.4) | async-done | bytes 2097184 | tf_op jit(solution)/shard_map/all_to_all | solution.py:100
  486.2 4.5 all-to-all-start.5
  490.8 2.5 slice.7
  493.3 4.4 copy.67
  497.7 4.9 all_to_all.105
  502.6 80.6 %all-to-all-done.5 = f32[8,128,1024]{2,1,0:T(8,128)} async-done(((f32[8,128,1024]{2,1,0:T(8,128)}), f32[8,128,1024]{2,1,0:T(8,128)}, u32[]{:S(2)}, u32[]{:S(2)}) %all-to-all-start.5) | async-done | bytes 4194336 | tf_op jit(solution)/shard_map/all_to_all | solution.py:102
  583.1 4.6 all-to-all-start.6
  587.7 2.4 copy.64
  590.2 4.1 copy.69
  594.2 5.1 copy.90
  599.4 3.2 reduce_sum.36
  603.6 76.6 %all-to-all-done.6 = f32[8,128,1024]{2,1,0:T(8,128)} async-done(((f32[8,128,1024]{2,1,0:T(8,128)}), f32[8,128,1024]{2,1,0:T(8,128)}, u32[]{:S(2)}, u32[]{:S(2)}) %all-to-all-start.6) | async-done | bytes 4194336 | tf_op jit(solution)/shard_map/all_to_all | solution.py:103
  680.2 5.2 copy.91
  685.4 3.2 reduce_sum.37
  688.8 0.9 copy.71
  (36 shorter events, 5.2 us)
Async XLA Ops:
  0.6 1.0 copy-start
  1.9 9.6 %copy-start.4 = (bf16[128,1024]{1,0:T(8,128)(2,1)S(1)}, bf16[128,1024]{1,0:T(8,128)(2,1)}, u32[]{:S(2)}) copy-start(bf16[128,1024]{1,0:T(8,128)(2,1)} %param.9) | copy-start | bytes 786436
  4.2 55.5 %all-to-all-start.1 = ((bf16[128,8,1024]{2,0,1:T(8,128)(2,1)}), bf16[128,8,1024]{2,0,1:T(8,128)(2,1)S(1)}, u32[]{:S(2)}, u32[]{:S(2)}) async-start(bf16[128,8,1024]{2,0,1:T(8,128)(2,1)} %all_to_all.89), calls=%async_computation.1 | async-start | bytes 4194304 | tf_op jit(solution)/shard_map/all_to_all | solution.py:60
  59.7 52.2 %all-to-all-start.3 = ((bf16[128,8,1024]{2,0,1:T(8,128)(2,1)}), bf16[128,8,1024]{2,0,1:T(8,128)(2,1)}, u32[]{:S(2)}, u32[]{:S(2)}) async-start(bf16[128,8,1024]{2,0,1:T(8,128)(2,1)} %all_to_all.95), calls=%async_computation.3 | async-start | bytes 4194304 | tf_op jit(solution)/shard_map/all_to_all | solution.py:61
  111.9 52.2 %all-to-all-start = ((bf16[128,8,1024]{2,0,1:T(8,128)(2,1)}), bf16[128,8,1024]{2,0,1:T(8,128)(2,1)}, u32[]{:S(2)}, u32[]{:S(2)}) async-start(bf16[128,8,1024]{2,0,1:T(8,128)(2,1)} %bitcast.135), calls=%async_computation | async-start | bytes 4194304 | tf_op jit(solution)/shard_map/all_to_all | solution.py:58
  116.3 52.2 %copy-start.5 = (s32[128]{0:T(128)S(1)}, s32[128]{0:T(128)}, u32[]{:S(2)}) copy-start(s32[128]{0:T(128)} %param.11) | copy-start | bytes 1540
  164.1 69.2 %all-to-all-start.2 = ((bf16[128,8,1024]{2,0,1:T(8,128)(2,1)}), bf16[128,8,1024]{2,0,1:T(8,128)(2,1)}, u32[]{:S(2)}, u32[]{:S(2)}) async-start(bf16[128,8,1024]{2,0,1:T(8,128)(2,1)} %bitcast.134), calls=%async_computation.2 | async-start | bytes 4194304 | tf_op jit(solution)/shard_map/all_to_all | solution.py:59
  318.7 2.4 copy-start.2
  321.8 1.3 copy-start.3
  405.4 2.4 copy-start.2
  408.5 1.3 copy-start.3
  429.6 56.7 %all-to-all-start.4 = ((bf16[8,128,1024]{2,1,0:T(8,128)(2,1)}), bf16[8,128,1024]{2,1,0:T(8,128)(2,1)S(1)}, u32[]{:S(2)}, u32[]{:S(2)}) async-start(bf16[8,128,1024]{2,1,0:T(8,128)(2,1)} %all_to_all.98), calls=%async_computation.4 | async-start | bytes 4194304 | tf_op jit(solution)/shard_map/all_to_all | solution.py:100
  486.2 96.9 %all-to-all-start.5 = ((f32[8,128,1024]{2,1,0:T(8,128)}), f32[8,128,1024]{2,1,0:T(8,128)}, u32[]{:S(2)}, u32[]{:S(2)}) async-start(f32[8,128,1024]{2,1,0:T(8,128)} %all_to_all.102), calls=%async_computation.5 | async-start | bytes 8388608 | tf_op jit(solution)/shard_map/all_to_all | solution.py:102
  583.1 97.1 %all-to-all-start.6 = ((f32[8,128,1024]{2,1,0:T(8,128)}), f32[8,128,1024]{2,1,0:T(8,128)}, u32[]{:S(2)}, u32[]{:S(2)}) async-start(f32[8,128,1024]{2,1,0:T(8,128)} %all_to_all.105), calls=%async_computation.6 | async-start | bytes 8388608 | tf_op jit(solution)/shard_map/all_to_all | solution.py:103
  680.2 9.4 %copy-start.1 = (bf16[128,1024]{1,0:T(8,128)(2,1)S(1)}, bf16[128,1024]{1,0:T(8,128)(2,1)}, u32[]{:S(2)}) copy-start(bf16[128,1024]{1,0:T(8,128)(2,1)} %param.8) | copy-start | bytes 786436
where the time goes:
time: 700 us; the launch traced here: 690 us
  waiting for transfers between devices  323 us (46%)
  local copies, waits for them, and re-layouts  107 us (15%)
  matrix products  84.3 us (12%)
  other arithmetic  75.6 us (11%)
  blocking collectives  48.4 us (7%)
  starting transfers between devices  40.4 us (6%)
  loops' own time  10.4 us (1%)
    all_to_all x1, waiting for transfers between devices, body(): lax.all_to_all(key_seq, 'sp', split_axis=0, concat_axis=1, tiled=True)  80.6 us
    all_to_all x1, waiting for transfers between devices, body(): lax.all_to_all(value_seq, 'sp', split_axis=0, concat_axis=1, tiled=True)  76.6 us
    all_gather x1, blocking collectives, body(): all_ids = lax.all_gather(segment_ids, 'sp', axis=0, tiled=True)  48.4 us
    all_to_all x1, waiting for transfers between devices, body(): lax.all_to_all(values_wide, 'sp', split_axis=1, concat_axis=0, tiled=True)  44.7 us
    all_to_all x1, waiting for transfers between devices, body(): lax.all_to_all(queries, 'sp', split_axis=1, concat_axis=0, tiled=True)  44.6 us
    sub x2, other arithmetic, grad_core(): probs = jnp.exp(scores - row_max)  43.5 us
    all_to_all x1, waiting for transfers between devices, body(): lax.all_to_all(keys_wide, 'sp', split_axis=1, concat_axis=0, tiled=True)  42.4 us
    all_to_all x1, waiting for transfers between devices, body(): lax.all_to_all(query_seq, 'sp', split_axis=0, concat_axis=1, tiled=True)  33.9 us
  transfers between devices with their start and end apart: 7, of which 6 were waited for; matrix products, arithmetic and copies ran while one was open for 8% of the time, Pallas kernels for 0%

commit v1 on v0

v1 whole, which is shorter than its diff:
```python
import functools

import jax
import jax.numpy as jnp
from jax import lax
from jax.experimental import pallas as pl
from jax.experimental.pallas import tpu as pltpu
from jax.sharding import PartitionSpec as P

HEAD_DIM = 128
MOST = 512
REACH = 4
SLOTS = REACH + 1
LOG2E = 1.4426950408889634
NT = (((1,), (1,)), ((), ()))


def kernel(
    n, kv_count, group,
    q_ref, k_ref, v_ref, g_ref, ids_ref,
    dq_ref, dk_ref, dv_ref,
    kv, ids, bias, probs, grads, part, out_buf, in_buf,
    kv_send, kv_recv, back_send, back_recv, ids_send, ids_recv,
):
    me = lax.axis_index("sp")
    odd = lax.rem(me, 2) == 1
    tokens = q_ref.shape[0]
    span = SLOTS * tokens
    scale = HEAD_DIM ** (-0.5)
    up = me + 2 < n
    partner = jnp.where(odd, me - 1, me + 1)

    def kv_copy(c, src, dst, which, target):
        return pltpu.make_async_remote_copy(
            src_ref=kv.at[c, src],
            dst_ref=kv.at[c, dst],
            send_sem=kv_send.at[c, which],
            recv_sem=kv_recv.at[c, dst - 1],
            device_id={"sp": target},
            device_id_type=pl.DeviceIdType.MESH,
        )

    def back_copy(c, slot, target):
        return pltpu.make_async_remote_copy(
            src_ref=out_buf.at[c, slot - 1],
            dst_ref=in_buf.at[c, slot - 1],
            send_sem=back_send.at[c, slot - 1],
            recv_sem=back_recv.at[c, slot - 1],
            device_id={"sp": target},
            device_id_type=pl.DeviceIdType.MESH,
        )

    def ids_copy(d):
        return pltpu.make_async_remote_copy(
            src_ref=ids_ref,
            dst_ref=ids.at[d],
            send_sem=ids_send.at[d - 1],
            recv_sem=ids_recv.at[d - 1],
            device_id={"sp": me + d},
            device_id_type=pl.DeviceIdType.MESH,
        )

    barrier = pltpu.get_barrier_semaphore()
    for d in range(1, SLOTS):
        @pl.when(me >= d)
        def _():
            pl.semaphore_signal(
                barrier, inc=1, device_id={"sp": me - d}, device_id_type=pl.DeviceIdType.MESH
            )

        @pl.when(me + d < n)
        def _():
            pl.semaphore_signal(
                barrier, inc=1, device_id={"sp": me + d}, device_id_type=pl.DeviceIdType.MESH
            )

    def fill(c, _):
        cols = pl.ds(pl.multiple_of(c * HEAD_DIM, HEAD_DIM), HEAD_DIM)
        kv[c, 0, 0] = k_ref[:, cols]
        kv[c, 0, 1] = v_ref[:, cols]
        for d in range(1, SLOTS):
            @pl.when(me < d)
            def _():
                kv[c, d] = jnp.zeros((2, tokens, HEAD_DIM), kv.dtype)
        return 0

    lax.fori_loop(0, kv_count, fill, 0)
    ids[0] = ids_ref[...]
    for d in range(1, SLOTS):
        @pl.when(me < d)
        def _():
            ids[d] = jnp.full(ids_ref.shape, -1, jnp.int32)

    pl.semaphore_wait(barrier, jnp.minimum(me, REACH) + jnp.minimum(n - 1 - me, REACH))

    def send_own(c):
        @pl.when(up)
        def _():
            kv_copy(c, 0, 2, 0, me + 2).start()

        @pl.when(jnp.logical_not(odd))
        def _():
            kv_copy(c, 0, 1, 2, me + 1).start()

    for d in range(1, SLOTS):
        @pl.when(me + d < n)
        def _():
            ids_copy(d).start()

    ahead = min(2, kv_count)
    for c in range(ahead):
        send_own(c)

    for d in range(1, SLOTS):
        @pl.when(me >= d)
        def _():
            ids_copy(d).wait_recv()

    row = jnp.broadcast_to(ids[0, 0:1, :].astype(jnp.float32), (tokens, tokens))
    for d in range(SLOTS):
        col = jnp.broadcast_to(ids[d, 0:1, :].astype(jnp.float32), (tokens, tokens)).T
        same = col == row
        if d == 0:
            key_at = lax.broadcasted_iota(jnp.int32, (tokens, tokens), 0)
            query_at = lax.broadcasted_iota(jnp.int32, (tokens, tokens), 1)
            same = same & (key_at <= query_at)
        bias[d * tokens:(d + 1) * tokens, :] = jnp.where(same, 0.0, -1e30)

    def stack(ref, c, first, count):
        cols = [
            ref[:, pl.ds(pl.multiple_of((c * group + first + i) * HEAD_DIM, HEAD_DIM), HEAD_DIM)]
            for i in range(count)
        ]
        return jnp.concatenate(cols, axis=0)

    def compute(c):
        keys = kv[c, :, 0].reshape(span, HEAD_DIM)
        values = kv[c, :, 1].reshape(span, HEAD_DIM)
        for pair in range(group // 2):
            q_pair = stack(q_ref, c, 2 * pair, 2)
            g_pair = stack(g_ref, c, 2 * pair, 2)
            blocked = bias[...]
            s = lax.dot_general(keys, q_pair, NT, preferred_element_type=jnp.float32)
            s = s + jnp.concatenate([blocked, blocked], axis=1)
            top = jnp.max(s, axis=0, keepdims=True)
            e = jnp.exp2((s - top) * (scale * LOG2E))
            p = e * (1.0 / jnp.sum(e, axis=0, keepdims=True))
            dp = lax.dot_general(values, g_pair, NT, preferred_element_type=jnp.float32)
            delta = jnp.sum(p * dp, axis=0, keepdims=True)
            lanes = slice(pair * 2 * tokens, (pair + 1) * 2 * tokens)
            probs[:, lanes] = p.astype(jnp.bfloat16)
            grads[:, lanes] = (p * (dp - delta)).astype(jnp.bfloat16)
        dv = jnp.dot(probs[...], stack(g_ref, c, 0, group), preferred_element_type=jnp.float32)
        dk = scale * jnp.dot(
            grads[...], stack(q_ref, c, 0, group), preferred_element_type=jnp.float32
        )
        for d in range(SLOTS):
            for which, array in ((0, dk), (1, dv)):
                block = array[d * tokens:(d + 1) * tokens]
                if d <= 2:
                    part[c, d, which] = block
                else:
                    out_buf[c, d - 1, which] = block.astype(jnp.bfloat16)
        @pl.when(me >= 3)
        def _():
            back_copy(c, 3, me - 2).start()

        @pl.when(me >= 4)
        def _():
            back_copy(c, 4, me - 2).start()

        dq_t = scale * jnp.dot(keys.T, grads[...], preferred_element_type=jnp.float32)
        for h in range(group):
            cols = pl.ds(pl.multiple_of((c * group + h) * HEAD_DIM, HEAD_DIM), HEAD_DIM)
            dq_ref[:, cols] = dq_t[:, h * tokens:(h + 1) * tokens].T.astype(jnp.bfloat16)

    def step(t, _):
        @pl.when(t < kv_count)
        def _():
            @pl.when(t + ahead < kv_count)
            def _():
                send_own(t + ahead)

            @pl.when(me >= 2)
            def _():
                kv_copy(t, 0, 2, 0, me).wait_recv()

                @pl.when(up)
                def _():
                    kv_copy(t, 2, 4, 1, me + 2).start()

                @pl.when(odd)
                def _():
                    kv_copy(t, 2, 1, 2, me - 1).start()

        @pl.when((t >= 1) & (t - 1 < kv_count))
        def _():
            @pl.when(me >= 1)
            def _():
                kv_copy(t - 1, 0, 1, 2, me).wait_recv()

                @pl.when(up)
                def _():
                    kv_copy(t - 1, 1, 3, 3, me + 2).start()

        @pl.when((t >= 2) & (t - 2 < kv_count))
        def _():
            @pl.when(me >= 3)
            def _():
                kv_copy(t - 2, 1, 3, 3, me).wait_recv()

            @pl.when(me >= 4)
            def _():
                kv_copy(t - 2, 2, 4, 1, me).wait_recv()

            compute(t - 2)

        @pl.when((t >= 3) & (t - 3 < kv_count))
        def _():
            c = t - 3

            @pl.when(up & (me >= 1))
            def _():
                back_copy(c, 3, me).wait_recv()
                part[c, 1] += in_buf[c, 2].astype(jnp.float32)

            @pl.when(up & (me >= 2))
            def _():
                back_copy(c, 4, me).wait_recv()
                part[c, 2] += in_buf[c, 3].astype(jnp.float32)

            @pl.when(me >= 1)
            def _():
                out_buf[c, 0] = part[c, 1].astype(jnp.bfloat16)
                back_copy(c, 1, partner).start()

        @pl.when((t >= 4) & (t - 4 < kv_count))
        def _():
            c = t - 4

            @pl.when(odd & (me >= 3))
            def _():
                back_copy(c, 1, me).wait_recv()
                part[c, 2] += in_buf[c, 0].astype(jnp.float32)

            @pl.when(jnp.logical_not(odd))
            def _():
                back_copy(c, 1, me).wait_recv()
                part[c, 0] += in_buf[c, 0].astype(jnp.float32)

            @pl.when(me >= 2)
            def _():
                out_buf[c, 1] = part[c, 2].astype(jnp.bfloat16)
                back_copy(c, 2, me - 2).start()

        @pl.when(t >= 5)
        def _():
            c = t - 5

            @pl.when(up)
            def _():
                back_copy(c, 2, me).wait_recv()
                part[c, 0] += in_buf[c, 1].astype(jnp.float32)

            cols = pl.ds(pl.multiple_of(c * HEAD_DIM, HEAD_DIM), HEAD_DIM)
            dk_ref[:, cols] = part[c, 0, 0].astype(jnp.bfloat16)
            dv_ref[:, cols] = part[c, 0, 1].astype(jnp.bfloat16)

        return 0

    lax.fori_loop(0, kv_count + 5, step, 0)

    def drain(c, _):
        @pl.when(up)
        def _():
            kv_copy(c, 0, 2, 0, me).wait_send()

            @pl.when(me >= 2)
            def _():
                kv_copy(c, 2, 4, 1, me).wait_send()

            @pl.when(me >= 1)
            def _():
                kv_copy(c, 1, 3, 3, me).wait_send()

        @pl.when(jnp.logical_not(odd) | (me >= 3))
        def _():
            kv_copy(c, 0, 1, 2, me).wait_send()

        for slot in range(1, SLOTS):
            @pl.when(me >= slot)
            def _():
                back_copy(c, slot, me).wait_send()
        return 0

    lax.fori_loop(0, kv_count, drain, 0)
    for d in range(1, SLOTS):
        @pl.when(me + d < n)
        def _():
            ids_copy(d).wait_send()


def body(queries, key_heads, value_heads, out_grad, segment_ids):
    tokens, width = queries.shape
    kv_width = key_heads.shape[1]
    kv_count = kv_width // HEAD_DIM
    group = width // kv_width
    n = lax.axis_size("sp")
    assert -(-(MOST - 1) // tokens) == REACH and n % 2 == 0 and group % 2 == 0
    ids_rows = jnp.broadcast_to(segment_ids[None, :], (8, tokens))
    span = SLOTS * tokens
    vmem = pl.BlockSpec(memory_space=pltpu.VMEM)
    pairs = (kv_count, REACH, 2, tokens, HEAD_DIM)
    dma = pltpu.SemaphoreType.DMA
    elements = kv_count * group * tokens * span
    return pl.pallas_call(
        functools.partial(kernel, n, kv_count, group),
        out_shape=(
            jax.ShapeDtypeStruct((tokens, width), jnp.bfloat16),
            jax.ShapeDtypeStruct((tokens, kv_width), jnp.bfloat16),
            jax.ShapeDtypeStruct((tokens, kv_width), jnp.bfloat16),
        ),
        in_specs=[vmem] * 5,
        out_specs=(vmem, vmem, vmem),
        scratch_shapes=[
            pltpu.VMEM((kv_count, SLOTS, 2, tokens, HEAD_DIM), jnp.bfloat16),
            pltpu.VMEM((SLOTS, 8, tokens), jnp.int32),
            pltpu.VMEM((span, tokens), jnp.float32),
            pltpu.VMEM((span, group * tokens), jnp.bfloat16),
            pltpu.VMEM((span, group * tokens), jnp.bfloat16),
            pltpu.VMEM((kv_count, 3, 2, tokens, HEAD_DIM), jnp.float32),
            pltpu.VMEM(pairs, jnp.bfloat16),
            pltpu.VMEM(pairs, jnp.bfloat16),
            dma((kv_count, 4)),
            dma((kv_count, REACH)),
            dma((kv_count, REACH)),
            dma((kv_count, REACH)),
            dma((REACH,)),
            dma((REACH,)),
        ],
        compiler_params=pltpu.CompilerParams(
            collective_id=0, has_side_effects=True, vmem_limit_bytes=48 * 1024 * 1024
        ),
        cost_estimate=pl.CostEstimate(
            flops=10 * elements * HEAD_DIM,
            bytes_accessed=6 * tokens * width + 8 * tokens * kv_width,
            transcendentals=elements,
        ),
    )(queries, key_heads, value_heads, out_grad, ids_rows)


def solution(mesh):
    rows = P(("dp", "sp"), None)
    return jax.shard_map(
        body,
        mesh=mesh,
        in_specs=(rows, rows, rows, rows, P(("dp", "sp"))),
        out_specs=(rows, rows, rows),
        check_vma=False,
    )
```

time: 700 us -> 72.9 us (0.10); the launches traced: 690 us -> 72.7 us
  waiting for transfers between devices: 323 us -> 0 us
  local copies, waits for them, and re-layouts: 107 us -> 6.87 us
  matrix products: 84.3 us -> 0 us
  other arithmetic: 75.6 us -> 0 us
  Pallas kernels: 0 us -> 65.1 us
  blocking collectives: 48.4 us -> 0 us
  starting transfers between devices: 40.4 us -> 0 us
  loops' own time: 10.4 us -> 0 us
    all_to_all x7 -> x0, waiting for transfers between devices: 323 us -> none  [the longest x1 80.6 us: body(): lax.all_to_all(key_seq, 'sp', split_axis=0, concat_axis=1, tiled=True)]
    dot_general x10 -> x0, matrix products: 84.3 us -> none  [the longest x2 25.9 us: grad_core(): jnp.einsum('kgqj,kgqd->kjd', probs_low, grad_part, preferred_element_type...]
    pallas_call x0 -> x1, Pallas kernels: none -> 65.1 us  [body(): pl.pallas_call(functools.partial(kernel, n, kv_count, group), out_shape=(...]
    all_gather x1 -> x0, blocking collectives: 48.4 us -> none  [body(): all_ids = lax.all_gather(segment_ids, 'sp', axis=0, tiled=True)]
    sub x2 -> x0, other arithmetic: 43.5 us -> none  [grad_core(): probs = jnp.exp(scores - row_max)]
    all_to_all x7 -> x0, starting transfers between devices: 40.4 us -> none  [the longest x1 11 us: body(): lax.all_to_all(query_seq, 'sp', split_axis=0, concat_axis=1, tiled=True)]
    all_to_all x8 -> x0, local copies, waits for them, and re-layouts: 29.2 us -> none  [the longest x2 6.62 us: body(): lax.all_to_all(query_seq, 'sp', split_axis=0, concat_axis=1, tiled=True)]
    convert_element_type x2 -> x0, other arithmetic: 23 us -> none  [grad_core(): score_grads = (probs * (prob_grads - delta)).astype(jnp.bfloat16)]
  transfers between devices with their start and end apart: 7 -> 0, of which waited for: 6 -> 0; matrix products, arithmetic and copies ran while one was open for 8% -> 0% of each run, Pallas kernels for 0% -> 0%
where the time goes in v1:
time: 72.9 us; the launch traced here: 72.7 us
  Pallas kernels  65.1 us (89%)
  local copies, waits for them, and re-layouts  6.87 us (9%)
    pallas_call x1, Pallas kernels, body(): pl.pallas_call(functools.partial(kernel, n, kv_count, group), out_shape=(...  65.1 us
    unnamed x9, local copies, waits for them, and re-layouts  6.22 us

profile of v1, /device:TPU:0, one launch (start us, length us, event | category | flops | bytes accessed | tf_op | source)
XLA Modules:
  0.0 72.7 jit_solution(13511262643965206400)
XLA Ops:
  0.6 0.7 broadcast_in_dim.2.ids_ref
  1.3 0.0 copy-start
  1.3 1.6 %copy-done = bf16[128,8192]{1,0:T(8,128)(2,1)S(1)} copy-done((bf16[128,8192]{1,0:T(8,128)(2,1)S(1)}, bf16[128,8192]{1,0:T(8,128)(2,1)}, u32[]{:S(2)}) %copy-start) | copy-done | bytes 2097176
  2.9 0.0 copy-start.1
  2.9 0.9 %copy-done.1 = bf16[128,1024]{1,0:T(8,128)(2,1)S(1)} copy-done((bf16[128,1024]{1,0:T(8,128)(2,1)S(1)}, bf16[128,1024]{1,0:T(8,128)(2,1)}, u32[]{:S(2)}) %copy-start.1) | copy-done | bytes 262168
  3.8 0.0 copy-start.2
  3.8 0.9 %copy-done.2 = bf16[128,1024]{1,0:T(8,128)(2,1)S(1)} copy-done((bf16[128,1024]{1,0:T(8,128)(2,1)S(1)}, bf16[128,1024]{1,0:T(8,128)(2,1)}, u32[]{:S(2)}) %copy-start.2) | copy-done | bytes 262168
  4.8 65.1 %shard_map.76 = (bf16[128,8192]{1,0:T(8,128)(2,1)S(1)}, bf16[128,1024]{1,0:T(8,128)(2,1)S(1)}, bf16[128,1024]{1,0:T(8,128)(2,1)S(1)}) custom-call(bf16[128,8192]{1,0:T(8,128)(2,1)S(1)} %copy-done, bf16[128,1024]{1,0:T(8,128)(2,1)S(1)} %copy-done.1, bf16[128,1024]{1,0:T(8,128)(2,1)S(1)} %copy-done.2, bf16[128,8192]{1,0:T(8,128)(2,1)} %g_ref.1, ...), custom_call_target="tpu_custom_call" | custom-call | flops 6710886400 | bytes 7340032 | tf_op jit(solution)/shard_map/pallas_call | solution.py:316
  69.9 1.3 %copy.11 = bf16[128,8192]{1,0:T(8,128)(2,1)} copy(bf16[128,8192]{1,0:T(8,128)(2,1)S(1)} %get-tuple-element.6) | data formatting | bytes 4194304
  71.3 0.7 copy.12
  72.0 0.7 copy.13
Async XLA Ops:
  1.3 1.6 %copy-start = (bf16[128,8192]{1,0:T(8,128)(2,1)S(1)}, bf16[128,8192]{1,0:T(8,128)(2,1)}, u32[]{:S(2)}) copy-start(bf16[128,8192]{1,0:T(8,128)(2,1)} %q_ref.1) | copy-start | bytes 6291460
  2.9 0.9 %copy-start.1 = (bf16[128,1024]{1,0:T(8,128)(2,1)S(1)}, bf16[128,1024]{1,0:T(8,128)(2,1)}, u32[]{:S(2)}) copy-start(bf16[128,1024]{1,0:T(8,128)(2,1)} %k_ref.1) | copy-start | bytes 786436
  3.8 0.9 %copy-start.2 = (bf16[128,1024]{1,0:T(8,128)(2,1)S(1)}, bf16[128,1024]{1,0:T(8,128)(2,1)}, u32[]{:S(2)}) copy-start(bf16[128,1024]{1,0:T(8,128)(2,1)} %v_ref.1) | copy-start | bytes 786436

commit v2 on v1

--- a/solution.py
+++ b/solution.py
@@ -17,14 +17,15 @@
 
 def kernel(
     n, kv_count, group,
-    q_ref, k_ref, v_ref, g_ref, ids_ref,
+    q_hbm, k_hbm, v_hbm, g_hbm, ids_ref,
     dq_ref, dk_ref, dv_ref,
-    kv, ids, bias, probs, grads, part, out_buf, in_buf,
+    q_ref, g_ref, kv, ids, bias, scores, prods, probs, grads, part, out_buf, in_buf,
+    fetch_sem,
     kv_send, kv_recv, back_send, back_recv, ids_send, ids_recv,
 ):
     me = lax.axis_index("sp")
     odd = lax.rem(me, 2) == 1
-    tokens = q_ref.shape[0]
+    tokens = q_hbm.shape[0]
     span = SLOTS * tokens
     scale = HEAD_DIM ** (-0.5)
     up = me + 2 < n
@@ -74,10 +75,26 @@
                 barrier, inc=1, device_id={"sp": me + d}, device_id_type=pl.DeviceIdType.MESH
             )
 
+    def fetch(c, what):
+        if what < 2:
+            cols = pl.ds(pl.multiple_of(c * HEAD_DIM, HEAD_DIM), HEAD_DIM)
+            return pltpu.make_async_copy(
+                (k_hbm, v_hbm)[what].at[:, cols], kv.at[c, 0, what], fetch_sem.at[c, what]
+            )
+        width = group * HEAD_DIM
+        cols = pl.ds(pl.multiple_of(c * width, width), width)
+        source, target = ((q_hbm, q_ref), (g_hbm, g_ref))[what - 2]
+        return pltpu.make_async_copy(source.at[:, cols], target.at[c], fetch_sem.at[c, what])
+
+    def start_fetch(c, first):
+        fetch(c, first).start()
+        fetch(c, first + 1).start()
+        return 0
+
+    lax.fori_loop(0, kv_count, lambda c, _: start_fetch(c, 0), 0)
+    lax.fori_loop(0, kv_count, lambda c, _: start_fetch(c, 2), 0)
+
     def fill(c, _):
-        cols = pl.ds(pl.multiple_of(c * HEAD_DIM, HEAD_DIM), HEAD_DIM)
-        kv[c, 0, 0] = k_ref[:, cols]
-        kv[c, 0, 1] = v_ref[:, cols]
         for d in range(1, SLOTS):
             @pl.when(me < d)
             def _():
@@ -94,6 +111,9 @@
     pl.semaphore_wait(barrier, jnp.minimum(me, REACH) + jnp.minimum(n - 1 - me, REACH))
 
     def send_own(c):
+        fetch(c, 0).wait()
+        fetch(c, 1).wait()
+
         @pl.when(up)
         def _():
             kv_copy(c, 0, 2, 0, me + 2).start()
@@ -127,29 +147,52 @@
         bias[d * tokens:(d + 1) * tokens, :] = jnp.where(same, 0.0, -1e30)
 
     def stack(ref, c, first, count):
-        cols = [
-            ref[:, pl.ds(pl.multiple_of((c * group + first + i) * HEAD_DIM, HEAD_DIM), HEAD_DIM)]
-            for i in range(count)
-        ]
+        cols = [ref[c, :, (first + i) * HEAD_DIM:(first + i + 1) * HEAD_DIM] for i in range(count)]
         return jnp.concatenate(cols, axis=0)
 
+    def fold(array, combine):
+        rows = [array[8 * i:8 * (i + 1)] for i in range(array.shape[0] // 8)]
+        while len(rows) > 1:
+            rows = [combine(rows[i], rows[i + 1]) for i in range(0, len(rows), 2)]
+        return rows[0]
+
+    factor = scale * LOG2E
+    tile = 64
+
     def compute(c):
+        fetch(c, 2).wait()
+        fetch(c, 3).wait()
         keys = kv[c, :, 0].reshape(span, HEAD_DIM)
         values = kv[c, :, 1].reshape(span, HEAD_DIM)
         for pair in range(group // 2):
+            lanes = slice(pair * 2 * tokens, (pair + 1) * 2 * tokens)
             q_pair = stack(q_ref, c, 2 * pair, 2)
             g_pair = stack(g_ref, c, 2 * pair, 2)
-            blocked = bias[...]
-            s = lax.dot_general(keys, q_pair, NT, preferred_element_type=jnp.float32)
-            s = s + jnp.concatenate([blocked, blocked], axis=1)
-            top = jnp.max(s, axis=0, keepdims=True)
-            e = jnp.exp2((s - top) * (scale * LOG2E))
-            p = e * (1.0 / jnp.sum(e, axis=0, keepdims=True))
-            dp = lax.dot_general(values, g_pair, NT, preferred_element_type=jnp.float32)
-            delta = jnp.sum(p * dp, axis=0, keepdims=True)
-            lanes = slice(pair * 2 * tokens, (pair + 1) * 2 * tokens)
-            probs[:, lanes] = p.astype(jnp.bfloat16)
-            grads[:, lanes] = (p * (dp - delta)).astype(jnp.bfloat16)
+            s_all = lax.dot_general(keys, q_pair, NT, preferred_element_type=jnp.float32)
+            tops = []
+            for at in range(0, span, tile):
+                blocked = bias[at:at + tile, :]
+                s = s_all[at:at + tile] + jnp.concatenate([blocked, blocked], axis=1)
+                scores[at:at + tile, lanes] = s
+                tops.append(fold(s, jnp.maximum))
+            top = jnp.max(functools.reduce(jnp.maximum, tops), axis=0, keepdims=True) * factor
+            dp_all = lax.dot_general(values, g_pair, NT, preferred_element_type=jnp.float32)
+            sums, dots = [], []
+            for at in range(0, span, tile):
+                e = jnp.exp2(scores[at:at + tile, lanes] * factor - top)
+                dp = dp_all[at:at + tile]
+                scores[at:at + tile, lanes] = e
+                prods[at:at + tile, lanes] = dp
+                sums.append(fold(e, jnp.add))
+                dots.append(fold(e * dp, jnp.add))
+            total = jnp.sum(functools.reduce(jnp.add, sums), axis=0, keepdims=True)
+            inverse = 1.0 / total
+            delta = jnp.sum(functools.reduce(jnp.add, dots), axis=0, keepdims=True) * inverse
+            for at in range(0, span, tile):
+                p = scores[at:at + tile, lanes] * inverse
+                probs[at:at + tile, lanes] = p.astype(jnp.bfloat16)
+                ds = p * (prods[at:at + tile, lanes] - delta)
+                grads[at:at + tile, lanes] = ds.astype(jnp.bfloat16)
         dv = jnp.dot(probs[...], stack(g_ref, c, 0, group), preferred_element_type=jnp.float32)
         dk = scale * jnp.dot(
             grads[...], stack(q_ref, c, 0, group), preferred_element_type=jnp.float32
@@ -320,17 +363,22 @@
             jax.ShapeDtypeStruct((tokens, kv_width), jnp.bfloat16),
             jax.ShapeDtypeStruct((tokens, kv_width), jnp.bfloat16),
         ),
-        in_specs=[vmem] * 5,
+        in_specs=[pl.BlockSpec(memory_space=pltpu.HBM)] * 4 + [vmem],
         out_specs=(vmem, vmem, vmem),
         scratch_shapes=[
+            pltpu.VMEM((kv_count, tokens, group * HEAD_DIM), jnp.bfloat16),
+            pltpu.VMEM((kv_count, tokens, group * HEAD_DIM), jnp.bfloat16),
             pltpu.VMEM((kv_count, SLOTS, 2, tokens, HEAD_DIM), jnp.bfloat16),
             pltpu.VMEM((SLOTS, 8, tokens), jnp.int32),
             pltpu.VMEM((span, tokens), jnp.float32),
+            pltpu.VMEM((span, group * tokens), jnp.float32),
+            pltpu.VMEM((span, group * tokens), jnp.float32),
             pltpu.VMEM((span, group * tokens), jnp.bfloat16),
             pltpu.VMEM((span, group * tokens), jnp.bfloat16),
             pltpu.VMEM((kv_count, 3, 2, tokens, HEAD_DIM), jnp.float32),
             pltpu.VMEM(pairs, jnp.bfloat16),
             pltpu.VMEM(pairs, jnp.bfloat16),
+            dma((kv_count, 4)),
             dma((kv_count, 4)),
             dma((kv_count, REACH)),
             dma((kv_count, REACH)),

time: 72.9 us -> 71 us (0.974)
  Pallas kernels: 65.1 us -> 63.3 us
    pallas_call x1, Pallas kernels: 65.1 us -> 63.3 us  [body(): pl.pallas_call(functools.partial(kernel, n, kv_count, group), out_shape=(...]
where the time goes in v2:
time: 71 us; the launch traced here: 70.8 us
  Pallas kernels  63.3 us (89%)
  local copies, waits for them, and re-layouts  6.87 us (10%)
    pallas_call x1, Pallas kernels, body(): pl.pallas_call(functools.partial(kernel, n, kv_count, group), out_shape=(...  63.3 us
    unnamed x9, local copies, waits for them, and re-layouts  6.22 us

profile of v2, /device:TPU:0, one launch (start us, length us, event | category | flops | bytes accessed | tf_op | source)
XLA Modules:
  0.0 70.8 jit_solution(1566759615236237189)
XLA Ops:
  0.6 0.7 broadcast_in_dim.2.ids_ref
  1.3 0.0 copy-start
  1.3 1.6 %copy-done = bf16[128,8192]{1,0:T(8,128)(2,1)S(1)} copy-done((bf16[128,8192]{1,0:T(8,128)(2,1)S(1)}, bf16[128,8192]{1,0:T(8,128)(2,1)}, u32[]{:S(2)}) %copy-start) | copy-done | bytes 2097176
  2.9 0.0 copy-start.1
  2.9 0.9 %copy-done.1 = bf16[128,1024]{1,0:T(8,128)(2,1)S(1)} copy-done((bf16[128,1024]{1,0:T(8,128)(2,1)S(1)}, bf16[128,1024]{1,0:T(8,128)(2,1)}, u32[]{:S(2)}) %copy-start.1) | copy-done | bytes 262168
  3.8 0.0 copy-start.2
  3.8 0.9 %copy-done.2 = bf16[128,1024]{1,0:T(8,128)(2,1)S(1)} copy-done((bf16[128,1024]{1,0:T(8,128)(2,1)S(1)}, bf16[128,1024]{1,0:T(8,128)(2,1)}, u32[]{:S(2)}) %copy-start.2) | copy-done | bytes 262168
  4.8 63.3 %shard_map.76 = (bf16[128,8192]{1,0:T(8,128)(2,1)S(1)}, bf16[128,1024]{1,0:T(8,128)(2,1)S(1)}, bf16[128,1024]{1,0:T(8,128)(2,1)S(1)}) custom-call(bf16[128,8192]{1,0:T(8,128)(2,1)S(1)} %copy-done, bf16[128,1024]{1,0:T(8,128)(2,1)S(1)} %copy-done.1, bf16[128,1024]{1,0:T(8,128)(2,1)S(1)} %copy-done.2, bf16[128,8192]{1,0:T(8,128)(2,1)} %g_hbm.1, ...), custom_call_target="tpu_custom_call" | custom-call | flops 6710886400 | bytes 7340032 | tf_op jit(solution)/shard_map/pallas_call | solution.py:359
  68.1 1.3 %copy.11 = bf16[128,8192]{1,0:T(8,128)(2,1)} copy(bf16[128,8192]{1,0:T(8,128)(2,1)S(1)} %get-tuple-element.6) | data formatting | bytes 4194304
  69.4 0.7 copy.12
  70.1 0.7 copy.13
Async XLA Ops:
  1.3 1.6 %copy-start = (bf16[128,8192]{1,0:T(8,128)(2,1)S(1)}, bf16[128,8192]{1,0:T(8,128)(2,1)}, u32[]{:S(2)}) copy-start(bf16[128,8192]{1,0:T(8,128)(2,1)} %q_hbm.1) | copy-start | bytes 6291460
  2.9 0.9 %copy-start.1 = (bf16[128,1024]{1,0:T(8,128)(2,1)S(1)}, bf16[128,1024]{1,0:T(8,128)(2,1)}, u32[]{:S(2)}) copy-start(bf16[128,1024]{1,0:T(8,128)(2,1)} %k_hbm.1) | copy-start | bytes 786436
  3.8 0.9 %copy-start.2 = (bf16[128,1024]{1,0:T(8,128)(2,1)S(1)}, bf16[128,1024]{1,0:T(8,128)(2,1)}, u32[]{:S(2)}) copy-start(bf16[128,1024]{1,0:T(8,128)(2,1)} %v_hbm.1) | copy-start | bytes 786436

commit v3 on v2

--- a/solution.py
+++ b/solution.py
@@ -19,7 +19,7 @@
     n, kv_count, group,
     q_hbm, k_hbm, v_hbm, g_hbm, ids_ref,
     dq_ref, dk_ref, dv_ref,
-    q_ref, g_ref, kv, ids, bias, scores, prods, probs, grads, part, out_buf, in_buf,
+    q_ref, g_ref, kv, ids, own, bias, scores, prods, probs, grads, part, out_buf, in_buf,
     fetch_sem,
     kv_send, kv_recv, back_send, back_recv, ids_send, ids_recv,
 ):
@@ -136,15 +136,17 @@
         def _():
             ids_copy(d).wait_recv()
 
+    key_at = lax.broadcasted_iota(jnp.int32, (tokens, tokens), 0)
+    query_at = lax.broadcasted_iota(jnp.int32, (tokens, tokens), 1)
     row = jnp.broadcast_to(ids[0, 0:1, :].astype(jnp.float32), (tokens, tokens))
-    for d in range(SLOTS):
-        col = jnp.broadcast_to(ids[d, 0:1, :].astype(jnp.float32), (tokens, tokens)).T
-        same = col == row
-        if d == 0:
-            key_at = lax.broadcasted_iota(jnp.int32, (tokens, tokens), 0)
-            query_at = lax.broadcasted_iota(jnp.int32, (tokens, tokens), 1)
-            same = same & (key_at <= query_at)
-        bias[d * tokens:(d + 1) * tokens, :] = jnp.where(same, 0.0, -1e30)
+    own[...] = (key_at <= query_at).astype(jnp.float32)
+
+    def ids_of(d):
+        return jnp.broadcast_to(ids[d, 0:1, :].astype(jnp.float32), (tokens, tokens)).T
+
+    for d in range(REACH):
+        col = jnp.where(own[...] > 0.0, ids_of(0), ids_of(REACH)) if d == 0 else ids_of(d)
+        bias[d * tokens:(d + 1) * tokens, :] = jnp.where(col == row, 0.0, -1e30)
 
     def stack(ref, c, first, count):
         cols = [ref[c, :, (first + i) * HEAD_DIM:(first + i + 1) * HEAD_DIM] for i in range(count)]
@@ -158,41 +160,80 @@
 
     factor = scale * LOG2E
     tile = 64
+    last = REACH * tokens
+
+    def twice(array):
+        return jnp.concatenate([array, array], axis=1)
+
+    def merged(array, at):
+        block = array[at:at + tile]
+        if at < tokens:
+            block = jnp.where(
+                twice(own[at:at + tile, :]) > 0.0, block, array[last + at:last + at + tile]
+            )
+        return block
+
+    def put(ref, at, lanes, block):
+        if at < tokens:
+            mine = twice(own[at:at + tile, :]) > 0.0
+            ref[at:at + tile, lanes] = jnp.where(mine, block, 0.0).astype(jnp.bfloat16)
+            ref[last + at:last + at + tile, lanes] = jnp.where(mine, 0.0, block).astype(
+                jnp.bfloat16
+            )
+        else:
+            ref[at:at + tile, lanes] = block.astype(jnp.bfloat16)
+
+    def lanes_of(pair):
+        return slice(pair * 2 * tokens, (pair + 1) * 2 * tokens)
+
+    def score_pass(c, pair):
+        keys = kv[c, :, 0].reshape(span, HEAD_DIM)
+        q_pair = stack(q_ref, c, 2 * pair, 2)
+        s_all = lax.dot_general(keys, q_pair, NT, preferred_element_type=jnp.float32)
+        tops = []
+        for at in range(0, last, tile):
+            s = merged(s_all, at) + twice(bias[at:at + tile, :])
+            scores[at:at + tile, lanes_of(pair)] = s
+            tops.append(fold(s, jnp.maximum))
+        return jnp.max(functools.reduce(jnp.maximum, tops), axis=0, keepdims=True) * factor
+
+    def exp_pass(c, pair, top):
+        lanes = lanes_of(pair)
+        values = kv[c, :, 1].reshape(span, HEAD_DIM)
+        g_pair = stack(g_ref, c, 2 * pair, 2)
+        dp_all = lax.dot_general(values, g_pair, NT, preferred_element_type=jnp.float32)
+        sums, dots = [], []
+        for at in range(0, last, tile):
+            e = jnp.exp2(scores[at:at + tile, lanes] * factor - top)
+            dp = merged(dp_all, at)
+            scores[at:at + tile, lanes] = e
+            prods[at:at + tile, lanes] = dp
+            sums.append(fold(e, jnp.add))
+            dots.append(fold(e * dp, jnp.add))
+        inverse = 1.0 / jnp.sum(functools.reduce(jnp.add, sums), axis=0, keepdims=True)
+        delta = jnp.sum(functools.reduce(jnp.add, dots), axis=0, keepdims=True) * inverse
+        return inverse, delta
+
+    def grad_pass(pair, inverse, delta):
+        lanes = lanes_of(pair)
+        for at in range(0, last, tile):
+            p = scores[at:at + tile, lanes] * inverse
+            put(probs, at, lanes, p)
+            put(grads, at, lanes, p * (prods[at:at + tile, lanes] - delta))
 
     def compute(c):
         fetch(c, 2).wait()
         fetch(c, 3).wait()
+        pairs = group // 2
+        tops, rest = {}, {}
+        for at in range(pairs + 2):
+            if at < pairs:
+                tops[at] = score_pass(c, at)
+            if 1 <= at <= pairs:
+                rest[at - 1] = exp_pass(c, at - 1, tops[at - 1])
+            if at >= 2:
+                grad_pass(at - 2, *rest[at - 2])
         keys = kv[c, :, 0].reshape(span, HEAD_DIM)
-        values = kv[c, :, 1].reshape(span, HEAD_DIM)
-        for pair in range(group // 2):
-            lanes = slice(pair * 2 * tokens, (pair + 1) * 2 * tokens)
-            q_pair = stack(q_ref, c, 2 * pair, 2)
-            g_pair = stack(g_ref, c, 2 * pair, 2)
-            s_all = lax.dot_general(keys, q_pair, NT, preferred_element_type=jnp.float32)
-            tops = []
-            for at in range(0, span, tile):
-                blocked = bias[at:at + tile, :]
-                s = s_all[at:at + tile] + jnp.concatenate([blocked, blocked], axis=1)
-                scores[at:at + tile, lanes] = s
-                tops.append(fold(s, jnp.maximum))
-            top = jnp.max(functools.reduce(jnp.maximum, tops), axis=0, keepdims=True) * factor
-            dp_all = lax.dot_general(values, g_pair, NT, preferred_element_type=jnp.float32)
-            sums, dots = [], []
-            for at in range(0, span, tile):
-                e = jnp.exp2(scores[at:at + tile, lanes] * factor - top)
-                dp = dp_all[at:at + tile]
-                scores[at:at + tile, lanes] = e
-                prods[at:at + tile, lanes] = dp
-                sums.append(fold(e, jnp.add))
-                dots.append(fold(e * dp, jnp.add))
-            total = jnp.sum(functools.reduce(jnp.add, sums), axis=0, keepdims=True)
-            inverse = 1.0 / total
-            delta = jnp.sum(functools.reduce(jnp.add, dots), axis=0, keepdims=True) * inverse
-            for at in range(0, span, tile):
-                p = scores[at:at + tile, lanes] * inverse
-                probs[at:at + tile, lanes] = p.astype(jnp.bfloat16)
-                ds = p * (prods[at:at + tile, lanes] - delta)
-                grads[at:at + tile, lanes] = ds.astype(jnp.bfloat16)
         dv = jnp.dot(probs[...], stack(g_ref, c, 0, group), preferred_element_type=jnp.float32)
         dk = scale * jnp.dot(
             grads[...], stack(q_ref, c, 0, group), preferred_element_type=jnp.float32
@@ -370,9 +411,10 @@
             pltpu.VMEM((kv_count, tokens, group * HEAD_DIM), jnp.bfloat16),
             pltpu.VMEM((kv_count, SLOTS, 2, tokens, HEAD_DIM), jnp.bfloat16),
             pltpu.VMEM((SLOTS, 8, tokens), jnp.int32),
-            pltpu.VMEM((span, tokens), jnp.float32),
-            pltpu.VMEM((span, group * tokens), jnp.float32),
-            pltpu.VMEM((span, group * tokens), jnp.float32),
+            pltpu.VMEM((tokens, tokens), jnp.float32),
+            pltpu.VMEM((REACH * tokens, tokens), jnp.float32),
+            pltpu.VMEM((REACH * tokens, group * tokens), jnp.float32),
+            pltpu.VMEM((REACH * tokens, group * tokens), jnp.float32),
             pltpu.VMEM((span, group * tokens), jnp.bfloat16),
             pltpu.VMEM((span, group * tokens), jnp.bfloat16),
             pltpu.VMEM((kv_count, 3, 2, tokens, HEAD_DIM), jnp.float32),
@@ -387,7 +429,7 @@
             dma((REACH,)),
         ],
         compiler_params=pltpu.CompilerParams(
-            collective_id=0, has_side_effects=True, vmem_limit_bytes=48 * 1024 * 1024
+            collective_id=0, has_side_effects=True, vmem_limit_bytes=61 * 1024 * 1024
         ),
         cost_estimate=pl.CostEstimate(
             flops=10 * elements * HEAD_DIM,

time: 71 us -> 71.6 us (level)
  Pallas kernels: 63.3 us -> 65 us
  local copies, waits for them, and re-layouts: 6.87 us -> 5.81 us
    pallas_call x1, Pallas kernels: 63.3 us -> 65 us  [body(): pl.pallas_call(functools.partial(kernel, n, kv_count, group), out_shape=(...]
    unnamed x9 -> x7, local copies, waits for them, and re-layouts: 6.22 us -> 4.56 us
where the time goes in v3:
time: 71.6 us; the launch traced here: 71.4 us
  Pallas kernels  65 us (91%)
  local copies, waits for them, and re-layouts  5.81 us (8%)
    pallas_call x1, Pallas kernels, body(): pl.pallas_call(functools.partial(kernel, n, kv_count, group), out_shape=(...  65 us
    unnamed x7, local copies, waits for them, and re-layouts  4.56 us

profile of v3, /device:TPU:0, one launch (start us, length us, event | category | flops | bytes accessed | tf_op | source)
XLA Modules:
  0.0 71.4 jit_solution(5882255234349598873)
XLA Ops:
  0.6 1.2 %broadcast_in_dim.2.ids_ref = s32[8,128]{1,0:T(8,128)} broadcast(s32[128]{0:T(128)} %param.9), dimensions={1} | broadcast | bytes 4608 | tf_op jit(solution)/shard_map/broadcast_in_dim | solution.py:394
  1.9 65.0 %shard_map.76 = (bf16[128,8192]{1,0:T(8,128)(2,1)}, bf16[128,1024]{1,0:T(8,128)(2,1)}, bf16[128,1024]{1,0:T(8,128)(2,1)}) custom-call(bf16[128,8192]{1,0:T(8,128)(2,1)} %q_hbm.1, bf16[128,1024]{1,0:T(8,128)(2,1)} %k_hbm.1, bf16[128,1024]{1,0:T(8,128)(2,1)} %v_hbm.1, bf16[128,8192]{1,0:T(8,128)(2,1)} %g_hbm.1, s32[8,128]{1,0:T(8,128)} %broadcast_in_dim.2.ids_ref), custom_call_target="tpu_custom_call" | custom-call | flops 6710886400 | bytes 7340032 | tf_op jit(solution)/shard_map/pallas_call | solution.py:400
  66.8 0.0 copy-start.1
  66.9 0.0 copy-start
  66.9 3.2 %copy.11 = bf16[128,8192]{1,0:T(8,128)(2,1)} copy(bf16[128,8192]{1,0:T(8,128)(2,1)} %get-tuple-element.6) | data formatting | bytes 4194304
  70.0 0.0 copy-done.1
  70.0 0.7 copy.12
  70.7 0.0 copy-done
  70.7 0.7 copy.13
Async XLA Ops:
  66.8 3.2 %copy-start.1 = (bf16[128,1024]{1,0:T(8,128)(2,1)S(1)}, bf16[128,1024]{1,0:T(8,128)(2,1)}, u32[]{:S(2)}) copy-start(bf16[128,1024]{1,0:T(8,128)(2,1)} %get-tuple-element.7) | copy-start | bytes 786436
  66.9 3.9 %copy-start = (bf16[128,1024]{1,0:T(8,128)(2,1)S(1)}, bf16[128,1024]{1,0:T(8,128)(2,1)}, u32[]{:S(2)}) copy-start(bf16[128,1024]{1,0:T(8,128)(2,1)} %get-tuple-element.8) | copy-start | bytes 786436

commit v4 on v3

--- a/solution.py
+++ b/solution.py
@@ -18,9 +18,9 @@
 def kernel(
     n, kv_count, group,
     q_hbm, k_hbm, v_hbm, g_hbm, ids_ref,
-    dq_ref, dk_ref, dv_ref,
+    dq_hbm, dk_hbm, dv_hbm,
     q_ref, g_ref, kv, ids, own, bias, scores, prods, probs, grads, part, out_buf, in_buf,
-    fetch_sem,
+    dq_ref, dkv_ref, fetch_sem, store_sem,
     kv_send, kv_recv, back_send, back_recv, ids_send, ids_recv,
 ):
     me = lax.axis_index("sp")
@@ -85,6 +85,16 @@
         cols = pl.ds(pl.multiple_of(c * width, width), width)
         source, target = ((q_hbm, q_ref), (g_hbm, g_ref))[what - 2]
         return pltpu.make_async_copy(source.at[:, cols], target.at[c], fetch_sem.at[c, what])
+
+    def store(c, what):
+        if what < 2:
+            cols = pl.ds(pl.multiple_of(c * HEAD_DIM, HEAD_DIM), HEAD_DIM)
+            source, target = dkv_ref.at[c, what], (dk_hbm, dv_hbm)[what].at[:, cols]
+        else:
+            width = group * HEAD_DIM
+            cols = pl.ds(pl.multiple_of(c * width, width), width)
+            source, target = dq_ref.at[c], dq_hbm.at[:, cols]
+        return pltpu.make_async_copy(source, target, store_sem.at[c, what])
 
     def start_fetch(c, first):
         fetch(c, first).start()
@@ -221,7 +231,7 @@
             put(probs, at, lanes, p)
             put(grads, at, lanes, p * (prods[at:at + tile, lanes] - delta))
 
-    def compute(c):
+    def first_half(c):
         fetch(c, 2).wait()
         fetch(c, 3).wait()
         pairs = group // 2
@@ -233,7 +243,8 @@
                 rest[at - 1] = exp_pass(c, at - 1, tops[at - 1])
             if at >= 2:
                 grad_pass(at - 2, *rest[at - 2])
-        keys = kv[c, :, 0].reshape(span, HEAD_DIM)
+
+    def second_half(c):
         dv = jnp.dot(probs[...], stack(g_ref, c, 0, group), preferred_element_type=jnp.float32)
         dk = scale * jnp.dot(
             grads[...], stack(q_ref, c, 0, group), preferred_element_type=jnp.float32
@@ -245,6 +256,7 @@
                     part[c, d, which] = block
                 else:
                     out_buf[c, d - 1, which] = block.astype(jnp.bfloat16)
+
         @pl.when(me >= 3)
         def _():
             back_copy(c, 3, me - 2).start()
@@ -253,106 +265,114 @@
         def _():
             back_copy(c, 4, me - 2).start()
 
+        keys = kv[c, :, 0].reshape(span, HEAD_DIM)
         dq_t = scale * jnp.dot(keys.T, grads[...], preferred_element_type=jnp.float32)
         for h in range(group):
-            cols = pl.ds(pl.multiple_of((c * group + h) * HEAD_DIM, HEAD_DIM), HEAD_DIM)
-            dq_ref[:, cols] = dq_t[:, h * tokens:(h + 1) * tokens].T.astype(jnp.bfloat16)
+            dq_ref[c, :, h * HEAD_DIM:(h + 1) * HEAD_DIM] = (
+                dq_t[:, h * tokens:(h + 1) * tokens].T.astype(jnp.bfloat16)
+            )
+        store(c, 2).start()
+
+    def within(c):
+        return (c >= 0) & (c < kv_count)
 
     def step(t, _):
-        @pl.when(t < kv_count)
-        def _():
-            @pl.when(t + ahead < kv_count)
-            def _():
-                send_own(t + ahead)
+        c = t - 2
+
+        @pl.when(within(t - 1) & (me >= 1))
+        def _():
+            kv_copy(t - 1, 0, 1, 2, me).wait_recv()
+
+            @pl.when(up)
+            def _():
+                kv_copy(t - 1, 1, 3, 3, me + 2).start()
+
+        @pl.when(within(t) & (me >= 2))
+        def _():
+            kv_copy(t, 0, 2, 0, me).wait_recv()
+
+            @pl.when(odd)
+            def _():
+                kv_copy(t, 2, 1, 2, me - 1).start()
+
+            @pl.when(up)
+            def _():
+                kv_copy(t, 2, 4, 1, me + 2).start()
+
+        @pl.when(within(c))
+        def _():
+            @pl.when(me >= 3)
+            def _():
+                kv_copy(c, 1, 3, 3, me).wait_recv()
+
+            @pl.when(me >= 4)
+            def _():
+                kv_copy(c, 2, 4, 1, me).wait_recv()
+
+            first_half(c)
+
+        @pl.when(t + ahead < kv_count)
+        def _():
+            send_own(t + ahead)
+
+        @pl.when(within(c - 2))
+        def _():
+            b = c - 2
+
+            @pl.when(up & (me >= 1))
+            def _():
+                back_copy(b, 3, me).wait_recv()
+                part[b, 1] += in_buf[b, 2].astype(jnp.float32)
+
+            @pl.when(up & (me >= 2))
+            def _():
+                back_copy(b, 4, me).wait_recv()
+                part[b, 2] += in_buf[b, 3].astype(jnp.float32)
+
+            @pl.when(me >= 1)
+            def _():
+                out_buf[b, 0] = part[b, 1].astype(jnp.bfloat16)
+                back_copy(b, 1, partner).start()
+
+        @pl.when(within(c - 3))
+        def _():
+            b = c - 3
+
+            @pl.when(odd & (me >= 3))
+            def _():
+                back_copy(b, 1, me).wait_recv()
+                part[b, 2] += in_buf[b, 0].astype(jnp.float32)
+
+            @pl.when(jnp.logical_not(odd))
+            def _():
+                back_copy(b, 1, me).wait_recv()
+                part[b, 0] += in_buf[b, 0].astype(jnp.float32)
 
             @pl.when(me >= 2)
             def _():
-                kv_copy(t, 0, 2, 0, me).wait_recv()
-
-                @pl.when(up)
-                def _():
-                    kv_copy(t, 2, 4, 1, me + 2).start()
-
-                @pl.when(odd)
-                def _():
-                    kv_copy(t, 2, 1, 2, me - 1).start()
-
-        @pl.when((t >= 1) & (t - 1 < kv_count))
-        def _():
-            @pl.when(me >= 1)
-            def _():
-                kv_copy(t - 1, 0, 1, 2, me).wait_recv()
-
-                @pl.when(up)
-                def _():
-                    kv_copy(t - 1, 1, 3, 3, me + 2).start()
-
-        @pl.when((t >= 2) & (t - 2 < kv_count))
-        def _():
-            @pl.when(me >= 3)
-            def _():
-                kv_copy(t - 2, 1, 3, 3, me).wait_recv()
-
-            @pl.when(me >= 4)
-            def _():
-                kv_copy(t - 2, 2, 4, 1, me).wait_recv()
-
-            compute(t - 2)
-
-        @pl.when((t >= 3) & (t - 3 < kv_count))
-        def _():
-            c = t - 3
-
-            @pl.when(up & (me >= 1))
-            def _():
-                back_copy(c, 3, me).wait_recv()
-                part[c, 1] += in_buf[c, 2].astype(jnp.float32)
-
-            @pl.when(up & (me >= 2))
-            def _():
-                back_copy(c, 4, me).wait_recv()
-                part[c, 2] += in_buf[c, 3].astype(jnp.float32)
-
-            @pl.when(me >= 1)
-            def _():
-                out_buf[c, 0] = part[c, 1].astype(jnp.bfloat16)
-                back_copy(c, 1, partner).start()
-
-        @pl.when((t >= 4) & (t - 4 < kv_count))
-        def _():
-            c = t - 4
-
-            @pl.when(odd & (me >= 3))
-            def _():
-                back_copy(c, 1, me).wait_recv()
-                part[c, 2] += in_buf[c, 0].astype(jnp.float32)
-
-            @pl.when(jnp.logical_not(odd))
-            def _():
-                back_copy(c, 1, me).wait_recv()
-                part[c, 0] += in_buf[c, 0].astype(jnp.float32)
-
-            @pl.when(me >= 2)
-            def _():
-                out_buf[c, 1] = part[c, 2].astype(jnp.bfloat16)
-                back_copy(c, 2, me - 2).start()
-
-        @pl.when(t >= 5)
-        def _():
-            c = t - 5
+                out_buf[b, 1] = part[b, 2].astype(jnp.bfloat16)
+                back_copy(b, 2, me - 2).start()
+
+        @pl.when(within(c - 5))
+        def _():
+            b = c - 5
 
             @pl.when(up)
             def _():
-                back_copy(c, 2, me).wait_recv()
-                part[c, 0] += in_buf[c, 1].astype(jnp.float32)
-
-            cols = pl.ds(pl.multiple_of(c * HEAD_DIM, HEAD_DIM), HEAD_DIM)
-            dk_ref[:, cols] = part[c, 0, 0].astype(jnp.bfloat16)
-            dv_ref[:, cols] = part[c, 0, 1].astype(jnp.bfloat16)
+                back_copy(b, 2, me).wait_recv()
+                part[b, 0] += in_buf[b, 1].astype(jnp.float32)
+
+            dkv_ref[b] = part[b, 0].astype(jnp.bfloat16)
+            store(b, 0).start()
+            store(b, 1).start()
+
+        @pl.when(within(c))
+        def _():
+            second_half(c)
 
         return 0
 
-    lax.fori_loop(0, kv_count + 5, step, 0)
+    lax.fori_loop(0, kv_count + 7, step, 0)
 
     def drain(c, _):
         @pl.when(up)
@@ -375,6 +395,8 @@
             @pl.when(me >= slot)
             def _():
                 back_copy(c, slot, me).wait_send()
+        for what in range(3):
+            store(c, what).wait()
         return 0
 
     lax.fori_loop(0, kv_count, drain, 0)
@@ -382,6 +404,23 @@
         @pl.when(me + d < n)
         def _():
             ids_copy(d).wait_send()
+
+
+def finish(dq_in, dk_in, dv_in, dq_out, dk_out, dv_out, sems):
+    tokens = dq_in.shape[0]
+    part = tokens // 4
+    copies = [
+        pltpu.make_async_copy(
+            dq_in.at[pl.ds(i * part, part)], dq_out.at[pl.ds(i * part, part)], sems.at[i]
+        )
+        for i in range(4)
+    ]
+    copies.append(pltpu.make_async_copy(dk_in, dk_out, sems.at[4]))
+    copies.append(pltpu.make_async_copy(dv_in, dv_out, sems.at[5]))
+    for copy in copies:
+        copy.start()
+    for copy in copies:
+        copy.wait()
 
 
 def body(queries, key_heads, value_heads, out_grad, segment_ids):
@@ -397,15 +436,17 @@
     pairs = (kv_count, REACH, 2, tokens, HEAD_DIM)
     dma = pltpu.SemaphoreType.DMA
     elements = kv_count * group * tokens * span
-    return pl.pallas_call(
+    shapes = (
+        jax.ShapeDtypeStruct((tokens, width), jnp.bfloat16),
+        jax.ShapeDtypeStruct((tokens, kv_width), jnp.bfloat16),
+        jax.ShapeDtypeStruct((tokens, kv_width), jnp.bfloat16),
+    )
+    anywhere = pl.BlockSpec(memory_space=pl.ANY)
+    grads = pl.pallas_call(
         functools.partial(kernel, n, kv_count, group),
-        out_shape=(
-            jax.ShapeDtypeStruct((tokens, width), jnp.bfloat16),
-            jax.ShapeDtypeStruct((tokens, kv_width), jnp.bfloat16),
-            jax.ShapeDtypeStruct((tokens, kv_width), jnp.bfloat16),
-        ),
+        out_shape=shapes,
         in_specs=[pl.BlockSpec(memory_space=pltpu.HBM)] * 4 + [vmem],
-        out_specs=(vmem, vmem, vmem),
+        out_specs=(anywhere, anywhere, anywhere),
         scratch_shapes=[
             pltpu.VMEM((kv_count, tokens, group * HEAD_DIM), jnp.bfloat16),
             pltpu.VMEM((kv_count, tokens, group * HEAD_DIM), jnp.bfloat16),
@@ -420,7 +461,10 @@
             pltpu.VMEM((kv_count, 3, 2, tokens, HEAD_DIM), jnp.float32),
             pltpu.VMEM(pairs, jnp.bfloat16),
             pltpu.VMEM(pairs, jnp.bfloat16),
+            pltpu.VMEM((kv_count, tokens, group * HEAD_DIM), jnp.bfloat16),
+            pltpu.VMEM((kv_count, 2, tokens, HEAD_DIM), jnp.bfloat16),
             dma((kv_count, 4)),
+            dma((kv_count, 3)),
             dma((kv_count, 4)),
             dma((kv_count, REACH)),
             dma((kv_count, REACH)),
@@ -437,6 +481,14 @@
             transcendentals=elements,
         ),
     )(queries, key_heads, value_heads, out_grad, ids_rows)
+    return pl.pallas_call(
+        finish,
+        out_shape=shapes,
+        in_specs=[anywhere] * 3,
+        out_specs=(anywhere, anywhere, anywhere),
+        scratch_shapes=[dma((6,))],
+        compiler_params=pltpu.CompilerParams(vmem_limit_bytes=61 * 1024 * 1024),
+    )(*grads)
 
 
 def solution(mesh):

time: 71.6 us -> 146 us (2.04)
  Pallas kernels: 65 us -> 144 us
  local copies, waits for them, and re-layouts: 5.81 us -> 1.25 us
    pallas_call x1 -> x2, Pallas kernels: 65 us -> 144 us  [the longest x1 80.6 us: body(): pl.pallas_call(finish, out_shape=shapes, in_specs=[anywhere] * 3, out_spe...]
    unnamed x7 -> x0, local copies, waits for them, and re-layouts: 4.56 us -> none
where the time goes in v4:
time: 146 us
  Pallas kernels  144 us (99%)
    pallas_call x1, Pallas kernels, body(): pl.pallas_call(finish, out_shape=shapes, in_specs=[anywhere] * 3, out_spe...  80.6 us
    pallas_call x1, Pallas kernels, body(): pl.pallas_call(functools.partial(kernel, n, kv_count, group), out_shape=s...  63.7 us

profile of v4, /device:TPU:0, one launch (start us, length us, event | category | flops | bytes accessed | tf_op | source)
XLA Modules:
  0.0 146.2 jit_solution(12044563218344605172)
XLA Ops:
  0.6 1.2 broadcast_in_dim.2.ids_ref
  1.9 63.7 %shard_map.76 = (bf16[128,8192]{1,0:T(8,128)(2,1)}, bf16[128,1024]{1,0:T(8,128)(2,1)}, bf16[128,1024]{1,0:T(8,128)(2,1)}) custom-call(bf16[128,8192]{1,0:T(8,128)(2,1)} %q_hbm.1, bf16[128,1024]{1,0:T(8,128)(2,1)} %k_hbm.1, bf16[128,1024]{1,0:T(8,128)(2,1)} %v_hbm.1, bf16[128,8192]{1,0:T(8,128)(2,1)} %g_hbm.1, s32[8,128]{1,0:T(8,128)} %broadcast_in_dim.2.ids_ref), custom_call_target="tpu_custom_call" | custom-call | flops 6710886400 | bytes 7340032 | tf_op jit(solution)/shard_map/pallas_call | solution.py:445
  65.6 80.6 %shard_map.77 = (bf16[128,8192]{1,0:T(8,128)(2,1)}, bf16[128,1024]{1,0:T(8,128)(2,1)}, bf16[128,1024]{1,0:T(8,128)(2,1)}) custom-call(bf16[128,8192]{1,0:T(8,128)(2,1)} %get-tuple-element.6.dq_in, bf16[128,1024]{1,0:T(8,128)(2,1)} %get-tuple-element.7.dk_in, bf16[128,1024]{1,0:T(8,128)(2,1)} %get-tuple-element.8.dv_in), custom_call_target="tpu_custom_call" | custom-call | tf_op jit(solution)/shard_map/pallas_call | solution.py:484

commit v5 on v4

--- a/solution.py
+++ b/solution.py
@@ -231,47 +231,43 @@
             put(probs, at, lanes, p)
             put(grads, at, lanes, p * (prods[at:at + tile, lanes] - delta))
 
-    def first_half(c):
-        fetch(c, 2).wait()
-        fetch(c, 3).wait()
-        pairs = group // 2
-        tops, rest = {}, {}
-        for at in range(pairs + 2):
-            if at < pairs:
-                tops[at] = score_pass(c, at)
-            if 1 <= at <= pairs:
-                rest[at - 1] = exp_pass(c, at - 1, tops[at - 1])
-            if at >= 2:
-                grad_pass(at - 2, *rest[at - 2])
-
-    def second_half(c):
+    def put_parts(c, which, array):
+        for d in range(SLOTS):
+            block = array[d * tokens:(d + 1) * tokens]
+            if d <= 2:
+                part[c, d, which] = block
+            else:
+                out_buf[c, d - 1, which] = block.astype(jnp.bfloat16)
+
+    def value_products(c):
         dv = jnp.dot(probs[...], stack(g_ref, c, 0, group), preferred_element_type=jnp.float32)
-        dk = scale * jnp.dot(
-            grads[...], stack(q_ref, c, 0, group), preferred_element_type=jnp.float32
-        )
-        for d in range(SLOTS):
-            for which, array in ((0, dk), (1, dv)):
-                block = array[d * tokens:(d + 1) * tokens]
-                if d <= 2:
-                    part[c, d, which] = block
-                else:
-                    out_buf[c, d - 1, which] = block.astype(jnp.bfloat16)
-
-        @pl.when(me >= 3)
-        def _():
-            back_copy(c, 3, me - 2).start()
-
-        @pl.when(me >= 4)
-        def _():
-            back_copy(c, 4, me - 2).start()
-
+        put_parts(c, 1, dv)
+
+    def key_products(c):
+        dk = jnp.dot(grads[...], stack(q_ref, c, 0, group), preferred_element_type=jnp.float32)
+        put_parts(c, 0, scale * dk)
+
+    def query_products(c):
         keys = kv[c, :, 0].reshape(span, HEAD_DIM)
         dq_t = scale * jnp.dot(keys.T, grads[...], preferred_element_type=jnp.float32)
         for h in range(group):
             dq_ref[c, :, h * HEAD_DIM:(h + 1) * HEAD_DIM] = (
                 dq_t[:, h * tokens:(h + 1) * tokens].T.astype(jnp.bfloat16)
             )
-        store(c, 2).start()
+
+    def compute(c, softmax, products):
+        pairs = group // 2
+        before = [value_products, key_products, query_products] if products else []
+        tops, rest = {}, {}
+        for at in range(pairs + 3):
+            if softmax and at < pairs:
+                tops[at] = score_pass(c, at)
+            if before:
+                before.pop(0)(c - 1)
+            if softmax and 1 <= at <= pairs:
+                rest[at - 1] = exp_pass(c, at - 1, tops[at - 1])
+            if softmax and at >= 3:
+                grad_pass(at - 3, *rest[at - 3])
 
     def within(c):
         return (c >= 0) & (c < kv_count)
@@ -309,15 +305,40 @@
             def _():
                 kv_copy(c, 2, 4, 1, me).wait_recv()
 
-            first_half(c)
+            fetch(c, 2).wait()
+            fetch(c, 3).wait()
+
+        @pl.when(c == 0)
+        def _():
+            compute(c, True, False)
+
+        @pl.when((c >= 1) & (c < kv_count))
+        def _():
+            compute(c, True, True)
+
+        @pl.when(c == kv_count)
+        def _():
+            compute(c, False, True)
+
+        @pl.when(within(c - 1))
+        def _():
+            @pl.when(me >= 3)
+            def _():
+                back_copy(c - 1, 3, me - 2).start()
+
+            @pl.when(me >= 4)
+            def _():
+                back_copy(c - 1, 4, me - 2).start()
+
+            store(c - 1, 2).start()
 
         @pl.when(t + ahead < kv_count)
         def _():
             send_own(t + ahead)
 
-        @pl.when(within(c - 2))
-        def _():
-            b = c - 2
+        @pl.when(within(c - 3))
+        def _():
+            b = c - 3
 
             @pl.when(up & (me >= 1))
             def _():
@@ -334,9 +355,9 @@
                 out_buf[b, 0] = part[b, 1].astype(jnp.bfloat16)
                 back_copy(b, 1, partner).start()
 
-        @pl.when(within(c - 3))
-        def _():
-            b = c - 3
+        @pl.when(within(c - 4))
+        def _():
+            b = c - 4
 
             @pl.when(odd & (me >= 3))
             def _():
@@ -353,9 +374,9 @@
                 out_buf[b, 1] = part[b, 2].astype(jnp.bfloat16)
                 back_copy(b, 2, me - 2).start()
 
-        @pl.when(within(c - 5))
-        def _():
-            b = c - 5
+        @pl.when(within(c - 6))
+        def _():
+            b = c - 6
 
             @pl.when(up)
             def _():
@@ -366,13 +387,9 @@
             store(b, 0).start()
             store(b, 1).start()
 
-        @pl.when(within(c))
-        def _():
-            second_half(c)
-
         return 0
 
-    lax.fori_loop(0, kv_count + 7, step, 0)
+    lax.fori_loop(0, kv_count + 8, step, 0)
 
     def drain(c, _):
         @pl.when(up)
@@ -406,21 +423,10 @@
             ids_copy(d).wait_send()
 
 
-def finish(dq_in, dk_in, dv_in, dq_out, dk_out, dv_out, sems):
-    tokens = dq_in.shape[0]
-    part = tokens // 4
-    copies = [
-        pltpu.make_async_copy(
-            dq_in.at[pl.ds(i * part, part)], dq_out.at[pl.ds(i * part, part)], sems.at[i]
-        )
-        for i in range(4)
-    ]
-    copies.append(pltpu.make_async_copy(dk_in, dk_out, sems.at[4]))
-    copies.append(pltpu.make_async_copy(dv_in, dv_out, sems.at[5]))
-    for copy in copies:
-        copy.start()
-    for copy in copies:
-        copy.wait()
+def finish(dq_in, dk_in, dv_in, dq_out, dk_out, dv_out):
+    dq_out[...] = dq_in[...]
+    dk_out[...] = dk_in[...]
+    dv_out[...] = dv_in[...]
 
 
 def body(queries, key_heads, value_heads, out_grad, segment_ids):
@@ -481,12 +487,15 @@
             transcendentals=elements,
         ),
     )(queries, key_heads, value_heads, out_grad, ids_rows)
+    blocks = tuple(
+        pl.BlockSpec((tokens // 4, shape.shape[1]), lambda i: (i, 0)) for shape in shapes
+    )
     return pl.pallas_call(
         finish,
         out_shape=shapes,
-        in_specs=[anywhere] * 3,
-        out_specs=(anywhere, anywhere, anywhere),
-        scratch_shapes=[dma((6,))],
+        grid=(4,),
+        in_specs=list(blocks),
+        out_specs=blocks,
         compiler_params=pltpu.CompilerParams(vmem_limit_bytes=61 * 1024 * 1024),
     )(*grads)
 

time: 146 us -> 73 us (0.50)
  Pallas kernels: 144 us -> 70.9 us
    pallas_call x1, Pallas kernels: 80.6 us -> 3.94 us  [body(): pl.pallas_call(finish, out_shape=shapes, grid=(4,), in_specs=list(blocks)...]
    pallas_call x1, Pallas kernels: 63.7 us -> 66.9 us  [body(): pl.pallas_call(functools.partial(kernel, n, kv_count, group), out_shape=s...]
where the time goes in v5:
time: 73 us; the launch traced here: 72.7 us
  Pallas kernels  70.9 us (97%)
  local copies, waits for them, and re-layouts  1.25 us (2%)
    pallas_call x1, Pallas kernels, body(): pl.pallas_call(functools.partial(kernel, n, kv_count, group), out_shape=s...  66.9 us
    pallas_call x1, Pallas kernels, body(): pl.pallas_call(finish, out_shape=shapes, grid=(4,), in_specs=list(blocks)...  3.94 us

profile of v5, /device:TPU:0, one launch (start us, length us, event | category | flops | bytes accessed | tf_op | source)
XLA Modules:
  0.0 72.7 jit_solution(5376797584511181220)
XLA Ops:
  0.6 1.2 %broadcast_in_dim.2.ids_ref = s32[8,128]{1,0:T(8,128)} broadcast(s32[128]{0:T(128)} %param.9), dimensions={1} | broadcast | bytes 4608 | tf_op jit(solution)/shard_map/broadcast_in_dim | solution.py:439
  1.9 66.9 %shard_map.76 = (bf16[128,8192]{1,0:T(8,128)(2,1)}, bf16[128,1024]{1,0:T(8,128)(2,1)}, bf16[128,1024]{1,0:T(8,128)(2,1)}) custom-call(bf16[128,8192]{1,0:T(8,128)(2,1)} %q_hbm.1, bf16[128,1024]{1,0:T(8,128)(2,1)} %k_hbm.1, bf16[128,1024]{1,0:T(8,128)(2,1)} %v_hbm.1, bf16[128,8192]{1,0:T(8,128)(2,1)} %g_hbm.1, s32[8,128]{1,0:T(8,128)} %broadcast_in_dim.2.ids_ref), custom_call_target="tpu_custom_call" | custom-call | flops 6710886400 | bytes 7340032 | tf_op jit(solution)/shard_map/pallas_call | solution.py:451
  68.8 3.9 %shard_map.77 = (bf16[128,8192]{1,0:T(8,128)(2,1)}, bf16[128,1024]{1,0:T(8,128)(2,1)}, bf16[128,1024]{1,0:T(8,128)(2,1)}) custom-call(bf16[128,8192]{1,0:T(8,128)(2,1)} %get-tuple-element.6.dq_in, bf16[128,1024]{1,0:T(8,128)(2,1)} %get-tuple-element.7.dk_in, bf16[128,1024]{1,0:T(8,128)(2,1)} %get-tuple-element.8.dv_in), custom_call_target="tpu_custom_call" | custom-call | tf_op jit(solution)/shard_map/pallas_call | solution.py:493

commit v6 on v4

--- a/solution.py
+++ b/solution.py
@@ -406,20 +406,26 @@
             ids_copy(d).wait_send()
 
 
-def finish(dq_in, dk_in, dv_in, dq_out, dk_out, dv_out, sems):
+def finish(dq_in, dk_in, dv_in, dq_out, dk_out, dv_out, dq_held, dk_held, dv_held, come, go):
     tokens = dq_in.shape[0]
     part = tokens // 4
-    copies = [
-        pltpu.make_async_copy(
-            dq_in.at[pl.ds(i * part, part)], dq_out.at[pl.ds(i * part, part)], sems.at[i]
-        )
-        for i in range(4)
+    moves = [(dq_in, dq_held, dq_out, pl.ds(i * part, part)) for i in range(4)]
+    moves.append((dk_in, dk_held, dk_out, pl.ds(0, tokens)))
+    moves.append((dv_in, dv_held, dv_out, pl.ds(0, tokens)))
+    first = [
+        pltpu.make_async_copy(source.at[rows], held.at[rows], come.at[i])
+        for i, (source, held, _, rows) in enumerate(moves)
     ]
-    copies.append(pltpu.make_async_copy(dk_in, dk_out, sems.at[4]))
-    copies.append(pltpu.make_async_copy(dv_in, dv_out, sems.at[5]))
-    for copy in copies:
+    second = [
+        pltpu.make_async_copy(held.at[rows], target.at[rows], go.at[i])
+        for i, (_, held, target, rows) in enumerate(moves)
+    ]
+    for copy in first:
         copy.start()
-    for copy in copies:
+    for before, after in zip(first, second):
+        before.wait()
+        after.start()
+    for copy in second:
         copy.wait()
 
 
@@ -430,7 +436,7 @@
     group = width // kv_width
     n = lax.axis_size("sp")
     assert -(-(MOST - 1) // tokens) == REACH and n % 2 == 0 and group % 2 == 0
-    ids_rows = jnp.broadcast_to(segment_ids[None, :], (8, tokens))
+    ids_rows = segment_ids.reshape(1, tokens)
     span = SLOTS * tokens
     vmem = pl.BlockSpec(memory_space=pltpu.VMEM)
     pairs = (kv_count, REACH, 2, tokens, HEAD_DIM)
@@ -451,7 +457,7 @@
             pltpu.VMEM((kv_count, tokens, group * HEAD_DIM), jnp.bfloat16),
             pltpu.VMEM((kv_count, tokens, group * HEAD_DIM), jnp.bfloat16),
             pltpu.VMEM((kv_count, SLOTS, 2, tokens, HEAD_DIM), jnp.bfloat16),
-            pltpu.VMEM((SLOTS, 8, tokens), jnp.int32),
+            pltpu.VMEM((SLOTS, 1, tokens), jnp.int32),
             pltpu.VMEM((tokens, tokens), jnp.float32),
             pltpu.VMEM((REACH * tokens, tokens), jnp.float32),
             pltpu.VMEM((REACH * tokens, group * tokens), jnp.float32),
@@ -486,7 +492,8 @@
         out_shape=shapes,
         in_specs=[anywhere] * 3,
         out_specs=(anywhere, anywhere, anywhere),
-        scratch_shapes=[dma((6,))],
+        scratch_shapes=[pltpu.VMEM(shape.shape, jnp.bfloat16) for shape in shapes]
+        + [dma((6,)), dma((6,))],
         compiler_params=pltpu.CompilerParams(vmem_limit_bytes=61 * 1024 * 1024),
     )(*grads)
 

time: 146 us -> 65.8 us (0.45)
  Pallas kernels: 144 us -> 65 us
    pallas_call x1, Pallas kernels: 80.6 us -> 2.63 us  [body(): pl.pallas_call(finish, out_shape=shapes, in_specs=[anywhere] * 3, out_spe...]
where the time goes in v6:
time: 65.8 us; the launch traced here: 65.7 us
  Pallas kernels  65 us (99%)
    pallas_call x1, Pallas kernels, body(): pl.pallas_call(functools.partial(kernel, n, kv_count, group), out_shape=s...  62.4 us
    pallas_call x1, Pallas kernels, body(): pl.pallas_call(finish, out_shape=shapes, in_specs=[anywhere] * 3, out_spe...  2.63 us

profile of v6, /device:TPU:0, one launch (start us, length us, event | category | flops | bytes accessed | tf_op | source)
XLA Modules:
  0.0 65.7 jit_solution(2747596301855887915)
XLA Ops:
  0.6 62.4 %shard_map.76 = (bf16[128,8192]{1,0:T(8,128)(2,1)}, bf16[128,1024]{1,0:T(8,128)(2,1)}, bf16[128,1024]{1,0:T(8,128)(2,1)}) custom-call(bf16[128,8192]{1,0:T(8,128)(2,1)} %q_hbm.1, bf16[128,1024]{1,0:T(8,128)(2,1)} %k_hbm.1, bf16[128,1024]{1,0:T(8,128)(2,1)} %v_hbm.1, bf16[128,8192]{1,0:T(8,128)(2,1)} %g_hbm.1, s32[1,128]{1,0:T(1,128)} %bitcast.1), custom_call_target="tpu_custom_call" | custom-call | flops 6710886400 | bytes 7340032 | tf_op jit(solution)/shard_map/pallas_call | solution.py:451
  63.0 2.6 %shard_map.77 = (bf16[128,8192]{1,0:T(8,128)(2,1)}, bf16[128,1024]{1,0:T(8,128)(2,1)}, bf16[128,1024]{1,0:T(8,128)(2,1)}) custom-call(bf16[128,8192]{1,0:T(8,128)(2,1)} %get-tuple-element.6.dq_in, bf16[128,1024]{1,0:T(8,128)(2,1)} %get-tuple-element.7.dk_in, bf16[128,1024]{1,0:T(8,128)(2,1)} %get-tuple-element.8.dv_in), custom_call_target="tpu_custom_call" | custom-call | tf_op jit(solution)/shard_map/pallas_call | solution.py:490

commit v7 on v6

--- a/solution.py
+++ b/solution.py
@@ -137,7 +137,7 @@
         def _():
             ids_copy(d).start()
 
-    ahead = min(2, kv_count)
+    ahead = min(3, kv_count)
     for c in range(ahead):
         send_own(c)
 

time: 65.8 us -> 67.1 us (1.020)
  Pallas kernels: 65 us -> 66.3 us
    pallas_call x1, Pallas kernels: 62.4 us -> 63.7 us  [body(): pl.pallas_call(functools.partial(kernel, n, kv_count, group), out_shape=s...]
where the time goes in v7:
time: 67.1 us; the launch traced here: 66.9 us
  Pallas kernels  66.3 us (99%)
    pallas_call x1, Pallas kernels, body(): pl.pallas_call(functools.partial(kernel, n, kv_count, group), out_shape=s...  63.7 us
    pallas_call x1, Pallas kernels, body(): pl.pallas_call(finish, out_shape=shapes, in_specs=[anywhere] * 3, out_spe...  2.63 us

profile of v7, /device:TPU:0, one launch (start us, length us, event | category | flops | bytes accessed | tf_op | source)
XLA Modules:
  0.0 66.9 jit_solution(4105785953453240732)
XLA Ops:
  0.6 63.7 %shard_map.76 = (bf16[128,8192]{1,0:T(8,128)(2,1)}, bf16[128,1024]{1,0:T(8,128)(2,1)}, bf16[128,1024]{1,0:T(8,128)(2,1)}) custom-call(bf16[128,8192]{1,0:T(8,128)(2,1)} %q_hbm.1, bf16[128,1024]{1,0:T(8,128)(2,1)} %k_hbm.1, bf16[128,1024]{1,0:T(8,128)(2,1)} %v_hbm.1, bf16[128,8192]{1,0:T(8,128)(2,1)} %g_hbm.1, s32[1,128]{1,0:T(1,128)} %bitcast.1), custom_call_target="tpu_custom_call" | custom-call | flops 6710886400 | bytes 7340032 | tf_op jit(solution)/shard_map/pallas_call | solution.py:451
  64.3 2.6 %shard_map.77 = (bf16[128,8192]{1,0:T(8,128)(2,1)}, bf16[128,1024]{1,0:T(8,128)(2,1)}, bf16[128,1024]{1,0:T(8,128)(2,1)}) custom-call(bf16[128,8192]{1,0:T(8,128)(2,1)} %get-tuple-element.6.dq_in, bf16[128,1024]{1,0:T(8,128)(2,1)} %get-tuple-element.7.dk_in, bf16[128,1024]{1,0:T(8,128)(2,1)} %get-tuple-element.8.dv_in), custom_call_target="tpu_custom_call" | custom-call | tf_op jit(solution)/shard_map/pallas_call | solution.py:490
